TPU v7x, 32 devices: a whole 2x2x4 slice. The times are simulated.
32 devices in a mesh: grp: 2 (over core), lat: 8 (over z, y), lon: 2 (over x).
Axes of the slice: x: 2, y: 2, z: 4, core: 2. Of those that a mesh axis runs over, the one named last changes fastest.
Arguments:
- control: float32 [64, 320, 1440], P('lon', ('grp', 'lat'))
- spectra: float32 [24, 64, 721], P(None, 'lon')
- band_starts: int32 [40], replicated, may hold values from 0 to 319, as said below
- band_spectrum: int32 [40], replicated, may hold values from 0 to 23, as said below
- shifts: int32 [2], replicated, may hold values from 1 to 9, as said below
- traj_start: bfloat16 [64, 320, 1440], P(None, ('grp', 'lat'), 'lon'), may hold values from -6 to 6
- traj_next: bfloat16 [64, 320, 1440], P(None, ('grp', 'lat'), 'lon'), may hold values from -6 to 6
- query_weight: bfloat16 [64, 256], replicated, may hold values from -0.75 to 0.75
- key_weight: bfloat16 [64, 256], replicated, may hold values from -0.75 to 0.75
- value_weight: bfloat16 [64, 256], replicated, may hold values from -0.75 to 0.75
- out_weight: bfloat16 [256, 64], replicated, may hold values from -0.75 to 0.75
- head_scale: float32 [4], replicated, may hold values from 2 to 12
- innov_one: float32 [64, 320, 1440], P(None, ('grp', 'lat'), 'lon'), may hold values from -6 to 6
- innov_two: float32 [64, 320, 1440], P(None, ('grp', 'lat'), 'lon'), may hold values from -6 to 6
- obs_weight_one: float32 [64, 320, 1440], P(None, ('grp', 'lat'), 'lon')
- obs_weight_two: float32 [64, 320, 1440], P(None, ('grp', 'lat'), 'lon')
- grad_prev: float32 [64, 320, 1440], P('lon', ('grp', 'lat'))
- dir_prev: float32 [64, 320, 1440], P('lon', ('grp', 'lat')), may hold values from -6 to 6
Outputs:
- gradient: float32 [64, 320, 1440], P('lon', ('grp', 'lat'))
- direction: float32 [64, 320, 1440], P('lon', ('grp', 'lat'))
- cost_value: float32 [], replicated
Inputs may be any that keep to these rules, and one draw needn't show every extreme that they name: Strictly increasing; the first is 0 and the last is 319; band b holds the rows from band_starts[b] up to the next start. `band_spectrum`: every entry of the table is used by some band. `shifts`: one of the two offsets is 9.
All inputs are finite; a program needn't handle non-finite values.
Results may differ from a plain program's by a relative error of at most 0.0025.
Values may be sent and summed in bfloat16 or wider, within the bound.
A program may use at most 320 MiB of HBM per device.

v0:
```python
import math

import jax
import jax.numpy as jnp
from jax import lax
from jax.sharding import PartitionSpec as P

WIN = 10


precise = lax.Precision.HIGHEST
triple_pass = lax.Precision.HIGH


def as_sent(shard):
    return jax.tree.map(lambda a: a.astype(jnp.bfloat16) if a.dtype == jnp.float32 else a, shard)


def from_behind(value, axis, steps):
    count = lax.axis_size(axis)
    pairs = [(source, (source + steps) % count) for source in range(count)]
    return lax.ppermute(value, axis, pairs)


def wave_tables(lon_len, wave_count):
    place = lax.broadcasted_iota(jnp.int32, (lon_len, wave_count), 0)
    wave = lax.broadcasted_iota(jnp.int32, (lon_len, wave_count), 1)
    angle = (place * wave % lon_len).astype(jnp.float32) * (2.0 * math.pi / lon_len)
    return (jnp.cos(angle), jnp.sin(angle))


def half_covariance(field, row_spec, cos_table, sin_table):
    fields_here, row_count, lon_len = field.shape
    wave_count = row_spec.shape[2]
    flat = field.reshape(-1, lon_len)
    real_part = jnp.dot(flat, cos_table, precision=triple_pass, preferred_element_type=jnp.float32)
    imag_part = jnp.dot(flat, sin_table, precision=triple_pass, preferred_element_type=jnp.float32)
    wave = lax.broadcasted_iota(jnp.int32, (1, wave_count), 1)
    weight = jnp.where((wave == 0) | (wave == lon_len // 2), 1.0, 2.0) / lon_len
    scaled = row_spec.reshape(-1, wave_count) * weight
    dims = (((1,), (1,)), ((), ()))
    restored = lax.dot_general(
        real_part * scaled,
        cos_table,
        dims,
        precision=triple_pass,
        preferred_element_type=jnp.float32,
    )
    restored = restored + lax.dot_general(
        imag_part * scaled,
        sin_table,
        dims,
        precision=triple_pass,
        preferred_element_type=jnp.float32,
    )
    return restored.reshape(fields_here, row_count, lon_len)


def to_tokens(field, win):
    depth, height, width = field.shape
    blocks = field.reshape(depth, height // win, win, width // win, win)
    return blocks.transpose(1, 3, 2, 4, 0).reshape(-1, win * win, depth)


def from_tokens(tokens, height, width, win):
    depth = tokens.shape[2]
    blocks = tokens.reshape(height // win, width // win, win, win, depth)
    return blocks.transpose(4, 0, 2, 1, 3).reshape(depth, height, width)


def unit_heads(projected, heads):
    shaped = projected.reshape(projected.shape[0], projected.shape[1], heads, -1)
    return (shaped * lax.rsqrt(jnp.sum(shaped * shaped, axis=-1, keepdims=True) + 1e-06)).astype(
        jnp.bfloat16
    )


def attention_weights(state, query_weight, key_weight, head_scale):
    tokens = to_tokens(state, WIN)
    heads = head_scale.shape[0]
    queries = unit_heads(
        jnp.einsum("ntc,cd->ntd", tokens, query_weight, preferred_element_type=jnp.float32), heads
    )
    keys_unit = unit_heads(
        jnp.einsum("ntc,cd->ntd", tokens, key_weight, preferred_element_type=jnp.float32), heads
    )
    scores = jnp.einsum("nthe,nshe->nhts", queries, keys_unit, preferred_element_type=jnp.float32)
    raised = jnp.exp(scores * head_scale[None, :, None, None])
    return (raised / jnp.sum(raised, axis=-1, keepdims=True)).astype(jnp.bfloat16)


def window_forward(field, weights, value_weight, out_weight):
    depth, height, width = field.shape
    tokens = to_tokens(field, WIN)
    count, span, heads = (tokens.shape[0], tokens.shape[1], weights.shape[1])
    values = jnp.einsum(
        "ntc,cd->ntd", tokens.astype(jnp.bfloat16), value_weight, preferred_element_type=jnp.float32
    )
    values = values.astype(jnp.bfloat16).reshape(count, span, heads, -1)
    mixed = jnp.einsum("nhts,nshe->nthe", weights, values, preferred_element_type=jnp.float32)
    mixed = mixed.astype(jnp.bfloat16).reshape(count, span, -1)
    result = tokens + jnp.einsum(
        "ntd,dc->ntc", mixed, out_weight, preferred_element_type=jnp.float32
    )
    return from_tokens(result, height, width, WIN)


def window_adjoint(field, weights, value_weight, out_weight):
    depth, height, width = field.shape
    tokens = to_tokens(field, WIN)
    count, span, heads = (tokens.shape[0], tokens.shape[1], weights.shape[1])
    upward = jnp.einsum(
        "ntc,dc->ntd", tokens.astype(jnp.bfloat16), out_weight, preferred_element_type=jnp.float32
    )
    upward = upward.astype(jnp.bfloat16).reshape(count, span, heads, -1)
    spread_back = jnp.einsum("nhts,nthe->nshe", weights, upward, preferred_element_type=jnp.float32)
    spread_back = spread_back.astype(jnp.bfloat16).reshape(count, span, -1)
    result = tokens + jnp.einsum(
        "ntd,cd->ntc", spread_back, value_weight, preferred_element_type=jnp.float32
    )
    return from_tokens(result, height, width, WIN)


def roll_ahead(field, shifts):
    depth, height, width = field.shape
    below = from_behind(as_sent(field[:, :WIN, :]), ("grp", "lat"), -1)
    moved = lax.dynamic_slice_in_dim(jnp.concatenate([field, below], axis=1), shifts[0], height, 1)
    beside = from_behind(as_sent(moved[:, :, :WIN]), "lon", -1)
    return lax.dynamic_slice_in_dim(jnp.concatenate([moved, beside], axis=2), shifts[1], width, 2)


def roll_behind(field, shifts):
    depth, height, width = field.shape
    above = from_behind(as_sent(field[:, height - WIN :, :]), ("grp", "lat"), 1)
    moved = lax.dynamic_slice_in_dim(
        jnp.concatenate([above, field], axis=1), WIN - shifts[0], height, 1
    )
    beside = from_behind(as_sent(moved[:, :, width - WIN :]), "lon", 1)
    return lax.dynamic_slice_in_dim(
        jnp.concatenate([beside, moved], axis=2), WIN - shifts[1], width, 2
    )


def trajectory_ahead(state, shifts):
    depth, height, width = state.shape
    below = from_behind(state[:, :WIN, :], ("grp", "lat"), -1)
    moved = lax.dynamic_slice_in_dim(jnp.concatenate([state, below], axis=1), shifts[0], height, 1)
    beside = from_behind(moved[:, :, :WIN], "lon", -1)
    return lax.dynamic_slice_in_dim(jnp.concatenate([moved, beside], axis=2), shifts[1], width, 2)


def body(
    control,
    spectra,
    band_starts,
    band_spectrum,
    shifts,
    traj_start,
    traj_next,
    query_weight,
    key_weight,
    value_weight,
    out_weight,
    head_scale,
    innov_one,
    innov_two,
    obs_weight_one,
    obs_weight_two,
    grad_prev,
    dir_prev,
):
    fields_here, row_count, lon_len = control.shape
    spec_count, wave_count = (spectra.shape[0], spectra.shape[2])
    first_row = lax.axis_index(("grp", "lat")) * row_count
    global_rows = first_row + jnp.arange(row_count, dtype=jnp.int32)
    band_of_row = (
        jnp.sum((band_starts[None, :] <= global_rows[:, None]).astype(jnp.int32), axis=1) - 1
    )
    band_hits = band_of_row[:, None] == jnp.arange(band_starts.shape[0], dtype=jnp.int32)[None, :]
    spec_of_row = jnp.sum(jnp.where(band_hits, band_spectrum[None, :], 0), axis=1)
    selector = (spec_of_row[:, None] == jnp.arange(spec_count, dtype=jnp.int32)[None, :]).astype(
        jnp.float32
    )
    row_spec = jnp.einsum(
        "rs,sfk->frk", selector, spectra, precision=precise, preferred_element_type=jnp.float32
    )
    cos_table, sin_table = wave_tables(lon_len, wave_count)
    prior_part = jnp.sum(control * control)
    previous_part = jnp.sum(grad_prev * grad_prev)
    prior, previous = lax.psum((prior_part, previous_part), ("grp", "lat", "lon"))
    start_cycle = half_covariance(control, row_spec, cos_table, sin_table)
    increment_start = lax.all_to_all(
        start_cycle.astype(jnp.bfloat16), "lon", split_axis=2, concat_axis=0, tiled=True
    ).astype(start_cycle.dtype)
    weights_start = attention_weights(traj_start, query_weight, key_weight, head_scale)
    increment_one = window_forward(increment_start, weights_start, value_weight, out_weight)
    weights_next = attention_weights(
        trajectory_ahead(traj_next, shifts), query_weight, key_weight, head_scale
    )
    increment_two = roll_behind(
        window_forward(roll_ahead(increment_one, shifts), weights_next, value_weight, out_weight),
        shifts,
    )
    misfit_one = increment_one - innov_one
    misfit_two = increment_two - innov_two
    misfit_part = jnp.sum(obs_weight_one * misfit_one * misfit_one) + jnp.sum(
        obs_weight_two * misfit_two * misfit_two
    )
    misfit = lax.psum(misfit_part, ("grp", "lat", "lon"))
    adjoint_two = obs_weight_two * misfit_two
    carried = roll_behind(
        window_adjoint(roll_ahead(adjoint_two, shifts), weights_next, value_weight, out_weight),
        shifts,
    )
    adjoint_one = carried + obs_weight_one * misfit_one
    adjoint_start = window_adjoint(adjoint_one, weights_start, value_weight, out_weight)
    back_cycle = lax.all_to_all(
        as_sent(adjoint_start), "lon", split_axis=0, concat_axis=2, tiled=True
    ).astype(adjoint_start.dtype)
    gradient = control + half_covariance(back_cycle, row_spec, cos_table, sin_table)
    current_part = jnp.sum(gradient * gradient)
    current = lax.psum(current_part, ("grp", "lat", "lon"))
    elements = fields_here * row_count * lon_len * lax.axis_size(("grp", "lat", "lon"))
    cost_value = 0.5 * (prior + misfit) / elements
    direction = -gradient + current / previous * dir_prev
    return (gradient, direction, cost_value)


def solution(mesh):
    in_specs = (
        P("lon", ("grp", "lat"), None),
        P(None, "lon", None),
        P(),
        P(),
        P(),
        P(None, ("grp", "lat"), "lon"),
        P(None, ("grp", "lat"), "lon"),
        P(),
        P(),
        P(),
        P(),
        P(),
        P(None, ("grp", "lat"), "lon"),
        P(None, ("grp", "lat"), "lon"),
        P(None, ("grp", "lat"), "lon"),
        P(None, ("grp", "lat"), "lon"),
        P("lon", ("grp", "lat"), None),
        P("lon", ("grp", "lat"), None),
    )
    out_specs = (P("lon", ("grp", "lat"), None), P("lon", ("grp", "lat"), None), P())
    return jax.shard_map(body, mesh=mesh, in_specs=in_specs, out_specs=out_specs, check_vma=False)
```

profile of v0, /device:TPU:12, one launch (start us, length us, event | category | flops | bytes accessed | tf_op | source)
XLA Modules:
  0.0 1359.9 jit_solution(3873376678102815970)
XLA Ops:
  15.0 31.2 %fusion.31 = f32[721,640]{1,0:T(8,128)} fusion(f32[640,1440]{1,0:T(8,128)} %reshape.170), kind=kOutput, calls=%fused_computation.73 | convolution fusion | flops 3996185600 | bytes 5532160 | tf_op jit(solution)/shard_map/dot_general | solution.py:36
  46.2 29.8 %fusion.39 = f32[721,640]{1,0:T(8,128)} fusion(f32[640,1440]{1,0:T(8,128)S(1)} %copy-done.9), kind=kOutput, calls=%fused_computation.77 | convolution fusion | flops 3996185600 | bytes 5532160 | tf_op jit(solution)/shard_map/dot_general | solution.py:37
  83.9 25.3 %fusion.29 = f32[640,1440]{0,1:T(8,128)S(1)} fusion(f32[721,640]{1,0:T(8,128)} %fusion.31, f32[640,721]{0,1:T(8,128)} %copy.378, f32[721]{0:T(1024)S(1)} %select_multiply_fusion), kind=kOutput, calls=%fused_computation.72 | convolution fusion | flops 3997108736 | bytes 7380804 | tf_op jit(solution)/shard_map/dot_general | solution.py:42
  109.2 24.4 %add_convert_fusion.1 = bf16[640,1440]{0,1:T(8,128)(2,1)} fusion(f32[640,1440]{0,1:T(8,128)S(1)} %fusion.29, f32[721,640]{1,0:T(8,128)S(1)} %copy-done.24, f32[640,721]{0,1:T(8,128)S(1)} %copy-done.11, f32[721]{0:T(1024)S(1)} %select_multiply_fusion), kind=kOutput, calls=%fused_computation.85 | convolution fusion | flops 3998951936 | bytes 9224004 | tf_op jit(solution)/shard_map/dot_general | solution.py:49
  140.1 9.1 copy.380
  149.2 12.8 reshape.212
  177.9 15.1 %copy.388 = bf16[2,72,10,10,64]{1,0,4,3,2:T(2,128)(2,1)} copy(bf16[2,72,10,10,64]{4,3,1,2,0:T(8,128)(2,1)} %bitcast.168) | data formatting | bytes 3686400 | tf_op jit(solution)/shard_map/transpose | solution.py:62
  222.5 26.1 %fusion.2 = f32[144,4,100,100]{2,3,1,0:T(8,128)} fusion(f32[144,100,4,64]{1,3,2,0:T(8,128)} %get-tuple-element.43, f32[144,100,4,64]{1,3,2,0:T(8,128)} %get-tuple-element.41, f32[144,100,4]{1,2,0:T(4,128)S(1)} %get-tuple-element.45, f32[144,100,4]{1,2,0:T(4,128)S(1)} %get-tuple-element.46), kind=kOutput, calls=%fused_computation.22 | convolution fusion | flops 752025600 | bytes 52992000 | tf_op jit(solution)/shard_map/nthe,nshe->nhts/dot_general | solution.py:87
  257.3 13.6 reshape.213
  270.9 12.1 copy.482
  283.0 14.3 %convert_element_type.153 = bf16[64,2,10,72,10]{0,4,3,2,1:T(8,128)(2,1)} reshape(bf16[2,32,20,720]{1,0,3,2:T(2,128)(2,1)} %bitcast.164) | data formatting | bytes 3686400 | tf_op jit(solution)/shard_map/convert_element_type | solution.py:194
  297.3 15.1 %copy.383 = bf16[2,72,10,10,64]{1,0,4,3,2:T(2,128)(2,1)} copy(bf16[2,72,10,10,64]{4,3,1,2,0:T(8,128)(2,1)} %bitcast.169) | data formatting | bytes 3686400 | tf_op jit(solution)/shard_map/transpose | solution.py:62
  331.3 12.1 copy.386
  360.5 15.1 %copy.403 = bf16[2,72,10,10,64]{1,0,4,3,2:T(2,128)(2,1)} copy(bf16[2,72,10,10,64]{4,3,1,2,0:T(8,128)(2,1)} %bitcast.170) | data formatting | bytes 3686400 | tf_op jit(solution)/shard_map/transpose | solution.py:62
  389.9 10.0 multiply_reduce_fusion
  400.0 8.0 multiply_reduce_fusion.1
  408.1 34.5 %fusion.1 = (f32[144,4,100]{2,1,0:T(4,128)S(1)}, f32[144,4,100]{2,1,0:T(4,128)S(1)}, f32[144,4,100,100]{2,3,1,0:T(8,128)}) fusion(f32[4]{0:T(128)S(1)} %copy-done.18, f32[144,4,100,100]{2,3,1,0:T(8,128)} %fusion.2, f32[144,100,4,64]{1,3,2,0:T(8,128)} %get-tuple-element.37, f32[144,100,4]{1,2,0:T(4,128)S(1)} %get-tuple-element.47, ...), kind=kOutput, calls=%fused_computation.5 | convolution fusion | flops 774950400 | bytes 76492816 | tf_op jit(solution)/shard_map/nthe,nshe->nhts/dot_general | solution.py:87
  442.6 30.5 %divide_convert_fusion = (bf16[144,4,100,100]{2,3,1,0:T(8,128)(2,1)}, bf16[144,4,100,100]{2,3,1,0:T(8,128)(2,1)}) fusion(f32[144,4,100,100]{2,3,1,0:T(8,128)} %get-tuple-element.44, f32[144,4,100]{2,1,0:T(4,128)S(1)} %get-tuple-element.21, f32[4]{0:T(128)S(1)} %copy-done.18, f32[144,4,100]{2,1,0:T(4,128)S(1)} %get-tuple-element.22, f32[144,4,100,100]{2,3,1,0:T(8,128)} %fusion.2), kind=kLoop, calls=%fused_computation | loop fusion | flops 34560000 | bytes 69580816 | tf_op jit(solution)/shard_map/convert_element_type | solution.py:89
  473.1 13.2 convolution_convert_fusion.7
  494.1 8.4 copy.395
  502.5 9.0 reshape.178
  511.5 16.4 %copy.396 = f32[64,2,10,72,10]{0,4,3,2,1:T(8,128)} copy(f32[64,2,10,72,10]{3,1,0,4,2:T(2,128)} %bitcast.165) | data formatting | bytes 7372800 | tf_op jit(solution)/shard_map/transpose | solution.py:68
  527.9 10.6 reshape.179
  543.3 22.2 %collective-permute-done = bf16[64,10,720]{2,0,1:T(8,128)(2,1)S(1)} collective-permute-done((bf16[64,10,720]{2,0,1:T(8,128)(2,1)S(1)}, bf16[64,10,720]{2,0,1:T(8,128)(2,1)S(1)}, u32[]{:S(2)}, u32[]{:S(2)}) %collective-permute-start) | collective-permute-done | bytes 921632 | tf_op jit(solution)/shard_map/ppermute | solution.py:22
  582.3 9.8 reshape.180
  592.1 16.5 %copy.399 = f32[2,72,10,10,64]{1,0,4,3,2:T(2,128)} copy(f32[2,72,10,10,64]{4,3,1,2,0:T(8,128)} %bitcast.155) | data formatting | bytes 7372800 | tf_op jit(solution)/shard_map/transpose | solution.py:62
  608.6 8.6 reshape.181
  617.2 8.0 copy.410
  632.8 11.7 copy.401
  644.5 13.8 %convolution_convert_fusion.6 = bf16[144,4,64,100]{3,2,1,0:T(8,128)(2,1)} fusion(bf16[144,100,4,64]{1,3,2,0:T(8,128)(2,1)} %bitcast.149, bf16[144,4,100,100]{2,3,1,0:T(8,128)(2,1)} %get-tuple-element.32), kind=kOutput, calls=%fused_computation.55 | convolution fusion | flops 740966400 | bytes 26265600 | tf_op jit(solution)/shard_map/nhts,nshe->nthe/dot_general | solution.py:100
  666.0 8.4 copy.411
  674.5 9.0 reshape.186
  683.5 16.4 %copy.412 = f32[64,2,10,72,10]{0,4,3,2,1:T(8,128)} copy(f32[64,2,10,72,10]{3,1,0,4,2:T(2,128)} %bitcast.166) | data formatting | bytes 7372800 | tf_op jit(solution)/shard_map/transpose | solution.py:68
  699.9 10.6 reshape.187
  716.5 17.8 %collective-permute-done.4 = bf16[64,10,720]{2,0,1:T(8,128)(2,1)S(1)} collective-permute-done((bf16[64,10,720]{2,0,1:T(8,128)(2,1)S(1)}, bf16[64,10,720]{2,0,1:T(8,128)(2,1)S(1)}, u32[]{:S(2)}, u32[]{:S(2)}) %collective-permute-start.4) | collective-permute-done | bytes 921632 | tf_op jit(solution)/shard_map/ppermute | solution.py:22
  758.8 9.0 multiply_reduce_fusion.4
  775.1 18.7 %collective-permute-done.6 = bf16[64,10,720]{2,0,1:T(8,128)(2,1)S(1)} collective-permute-done((bf16[64,10,720]{2,0,1:T(8,128)(2,1)S(1)}, bf16[64,10,720]{2,0,1:T(8,128)(2,1)S(1)}, u32[]{:S(2)}, u32[]{:S(2)}) %collective-permute-start.6) | collective-permute-done | bytes 921632 | tf_op jit(solution)/shard_map/ppermute | solution.py:22
  810.9 9.8 reshape.188
  820.7 16.5 %copy.419 = f32[2,72,10,10,64]{1,0,4,3,2:T(2,128)} copy(f32[2,72,10,10,64]{4,3,1,2,0:T(8,128)} %bitcast.156) | data formatting | bytes 7372800 | tf_op jit(solution)/shard_map/transpose | solution.py:62
  837.2 8.6 reshape.189
  845.8 8.0 copy.424
  861.3 11.7 copy.421
  873.1 16.9 %convolution_convert_fusion.5 = bf16[144,4,64,100]{3,2,1,0:T(8,128)(2,1)} fusion(bf16[144,100,4,64]{1,3,2,0:T(8,128)(2,1)} %bitcast.152, bf16[144,4,100,100]{2,3,1,0:T(8,128)(2,1)} %get-tuple-element.32), kind=kOutput, calls=%fused_computation.54 | convolution fusion | flops 740966400 | bytes 26265600 | tf_op jit(solution)/shard_map/nhts,nthe->nshe/dot_general | solution.py:116
  897.6 8.4 copy.425
  906.1 9.0 reshape.192
  915.1 16.4 %copy.426 = f32[64,2,10,72,10]{0,4,3,2,1:T(8,128)} copy(f32[64,2,10,72,10]{3,1,0,4,2:T(2,128)} %bitcast.167) | data formatting | bytes 7372800 | tf_op jit(solution)/shard_map/transpose | solution.py:68
  931.5 10.6 reshape.193
  945.4 19.8 %collective-permute-done.8 = bf16[64,10,720]{2,0,1:T(8,128)(2,1)S(1)} collective-permute-done((bf16[64,10,720]{2,0,1:T(8,128)(2,1)S(1)}, bf16[64,10,720]{2,0,1:T(8,128)(2,1)S(1)}, u32[]{:S(2)}, u32[]{:S(2)}) %collective-permute-start.8) | collective-permute-done | bytes 921632 | tf_op jit(solution)/shard_map/ppermute | solution.py:22
  988.2 14.3 %multiply_reduce_fusion.5 = (f32[]{:T(128)}, f32[64,20,720]{0,2,1:T(8,128)}) fusion(f32[64,20,720]{0,2,1:T(8,128)} %copy.430, f32[64,20,720]{0,2,1:T(8,128)} %reshape.179, f32[64,20,720]{0,2,1:T(8,128)} %copy.429, s32[]{:T(128)S(6)} %select_n.59, f32[64,20,720]{0,2,1:T(8,128)} %copy-done.5, f32[64,20,10]{0,2,1:T(8,128)S(1)} %convert_element_type.178), kind=kLoop, calls=%fused_computation.48 | loop fusion | flops 5529599 | bytes 18483208 | tf_op jit(solution)/shard_map/reduce_sum | solution.py:206
  1002.6 9.8 reshape.194
  1012.4 16.5 %copy.431 = f32[2,72,10,10,64]{1,0,4,3,2:T(2,128)} copy(f32[2,72,10,10,64]{4,3,1,2,0:T(8,128)} %bitcast.157) | data formatting | bytes 7372800 | tf_op jit(solution)/shard_map/transpose | solution.py:62
  1028.9 8.6 reshape.195
  1042.5 8.0 copy.436
  1061.9 11.8 copy.433
  1073.7 17.0 %convolution_convert_fusion.4 = bf16[144,4,64,100]{3,2,1,0:T(8,128)(2,1)} fusion(bf16[144,100,4,64]{1,3,2,0:T(8,128)(2,1)} %bitcast.153, bf16[144,4,100,100]{2,3,1,0:T(8,128)(2,1)} %get-tuple-element.33), kind=kOutput, calls=%fused_computation.53 | convolution fusion | flops 740966400 | bytes 26265600 | tf_op jit(solution)/shard_map/nhts,nthe->nshe/dot_general | solution.py:116
  1103.0 8.1 convert_element_type.184
  1111.1 14.5 %copy.438 = bf16[64,2,10,72,10]{0,4,3,2,1:T(8,128)(2,1)} copy(bf16[64,2,10,72,10]{3,1,0,4,2:T(2,128)(2,1)} %bitcast.173) | data formatting | bytes 3686400 | tf_op jit(solution)/shard_map/convert_element_type | solution.py:16
  1125.7 8.2 convert_element_type.186
  1150.9 15.3 %all-to-all-done.1 = bf16[64,20,720]{2,1,0:T(8,128)(2,1)S(1)} async-done(((bf16[64,20,720]{2,1,0:T(8,128)(2,1)}), bf16[64,20,720]{2,1,0:T(8,128)(2,1)S(1)}, u32[]{:S(2)}, u32[]{:S(2)}) %all-to-all-start.1) | async-done | bytes 1843232 | tf_op jit(solution)/shard_map/all_to_all | solution.py:217
  1174.5 20.0 %fusion.27 = f32[640,721]{0,1:T(8,128)S(1)} fusion(bf16[640,1440]{1,0:T(8,128)(2,1)S(1)} %reshape.198), kind=kOutput, calls=%fused_computation.71 | convolution fusion | flops 3996185600 | bytes 3688960 | tf_op jit(solution)/shard_map/dot_general | solution.py:36
  1194.5 20.1 %fusion.35 = f32[640,721]{0,1:T(8,128)S(1)} fusion(bf16[640,1440]{1,0:T(8,128)(2,1)S(1)} %reshape.198), kind=kOutput, calls=%fused_computation.75 | convolution fusion | flops 3996185600 | bytes 3688960 | tf_op jit(solution)/shard_map/dot_general | solution.py:37
  1214.7 23.0 %fusion.25 = f32[640,1440]{0,1:T(8,128)S(1)} fusion(f32[640,721]{0,1:T(8,128)S(1)} %fusion.27, f32[640,721]{0,1:T(8,128)S(1)} %copy-done.12, f32[721]{0:T(1024)S(1)} %copy-done.20), kind=kOutput, calls=%fused_computation.70 | convolution fusion | flops 3997108736 | bytes 7380804 | tf_op jit(solution)/shard_map/dot_general | solution.py:42
  1237.7 24.2 %fusion.44 = f32[640,1440]{0,1:T(8,128)} fusion(f32[640,1440]{0,1:T(8,128)S(1)} %fusion.25, f32[640,721]{0,1:T(8,128)S(1)} %fusion.35, f32[640,721]{0,1:T(8,128)S(1)} %copy-done.12, f32[721]{0:T(1024)S(1)} %copy-done.20), kind=kOutput, calls=%fused_computation.86 | convolution fusion | flops 3998030336 | bytes 11067204 | tf_op jit(solution)/shard_map/dot_general | solution.py:49
  1285.3 60.6 %all-reduce = (f32[]{:T(128)}, f32[]{:T(128)}, f32[]{:T(128)}) all-reduce(f32[]{:T(128)} %get-tuple-element.28, f32[]{:T(128)} %multiply_reduce_fusion.8, f32[]{:T(128)S(6)} %add.153), channel_id=1, replica_groups=mesh['grp'=2,'lat'=8,'lon'=2] {'grp','lat','lon'}, use_global_device_ids=true, to_apply=%region_9.10 | all-reduce | flops 3 | bytes 24 | tf_op jit(solution)/shard_map/psum | solution.py:222
  (169 shorter events, 353.6 us)
Async XLA Ops:
  0.6 75.7 %copy-start = (f32[24,32,721]{2,1,0:T(8,128)S(1)}, f32[24,32,721]{2,1,0:T(8,128)}, u32[]{:S(2)}) copy-start(f32[24,32,721]{2,1,0:T(8,128)} %param.19) | copy-start | bytes 6644740
  3.1 250.2 %collective-permute-start.2 = (bf16[64,10,720]{2,0,1:T(8,128)(2,1)}, bf16[64,10,720]{2,0,1:T(8,128)(2,1)S(1)}, u32[]{:S(2)}, u32[]{:S(2)}) collective-permute-start(bf16[64,10,720]{2,0,1:T(8,128)(2,1)} %slice.56), channel_id=1, source_target_pairs={{0,30},{2,0},{4,2},{6,4},{8,6},{10,8},{12,10},{14,12},{16,14},{18,... | collective-permute-start | bytes 2764808 | tf_op jit(solution)/shard_map/ppermute | solution.py:22
  3.6 105.6 %copy-start.19 = (f32[721]{0:T(1024)}, f32[721]{0:T(1024)S(1)}, u32[]{:S(2)}) copy-start(f32[721]{0:T(1024)S(1)} %select_multiply_fusion) | copy-start | bytes 8656
  15.0 31.2 %copy-start.9 = (f32[640,1440]{1,0:T(8,128)S(1)}, f32[640,1440]{1,0:T(8,128)}, u32[]{:S(2)}) copy-start(f32[640,1440]{1,0:T(8,128)} %reshape.170) | copy-start | bytes 11059204
  46.2 29.8 %copy-start.22 = (s32[40]{0:T(128)S(1)}, s32[40]{0:T(128)}, u32[]{:S(2)}) copy-start(s32[40]{0:T(128)} %param.20) | copy-start | bytes 484
  46.2 30.0 %copy-start.23 = (s32[40]{0:T(128)S(1)}, s32[40]{0:T(128)}, u32[]{:S(2)}) copy-start(s32[40]{0:T(128)} %param.21) | copy-start | bytes 484
  83.9 25.4 %copy-start.11 = (f32[640,721]{0,1:T(8,128)S(1)}, f32[640,721]{0,1:T(8,128)}, u32[]{:S(2)}) copy-start(f32[640,721]{0,1:T(8,128)} %copy.378) | copy-start | bytes 5537284
  83.9 25.4 %copy-start.24 = (f32[721,640]{1,0:T(8,128)S(1)}, f32[721,640]{1,0:T(8,128)}, u32[]{:S(2)}) copy-start(f32[721,640]{1,0:T(8,128)} %fusion.39) | copy-start | bytes 5537284
  149.2 17.7 %copy-start.16 = (bf16[64,256]{1,0:T(8,128)(2,1)S(1)}, bf16[64,256]{1,0:T(8,128)(2,1)}, u32[]{:S(2)}) copy-start(bf16[64,256]{1,0:T(8,128)(2,1)} %param.26) | copy-start | bytes 98308
  149.2 17.8 %copy-start.17 = (bf16[64,256]{1,0:T(8,128)(2,1)S(1)}, bf16[64,256]{1,0:T(8,128)(2,1)}, u32[]{:S(2)}) copy-start(bf16[64,256]{1,0:T(8,128)(2,1)} %param.25) | copy-start | bytes 98308
  162.1 5.1 copy-start.10
  162.1 95.2 %all-to-all-start = ((bf16[2,2,230400]{2,1,0:T(2,128)(2,1)}), bf16[2,2,230400]{2,1,0:T(2,128)(2,1)}, u32[]{:S(2)}, u32[]{:S(2)}) async-start(bf16[2,2,230400]{2,1,0:T(2,128)(2,1)} %reshape.212), calls=%async_computation | async-start | bytes 3686400 | tf_op jit(solution)/shard_map/all_to_all | solution.py:192
  222.5 26.1 %copy-start.21 = (s32[2]{0:T(128)S(1)}, s32[2]{0:T(128)}, u32[]{:S(2)}) copy-start(s32[2]{0:T(128)} %param.22) | copy-start | bytes 28
  255.2 15.7 %copy-start.7 = (bf16[64,20,720]{2,0,1:T(8,128)(2,1)}, bf16[64,20,720]{2,0,1:T(8,128)(2,1)S(1)}, u32[]{:S(2)}) copy-start(bf16[64,20,720]{2,0,1:T(8,128)(2,1)S(1)} %fusion.75) | copy-start | bytes 5529604
  255.2 88.2 %collective-permute-start.3 = (bf16[64,20,10]{2,0,1:T(8,128)(2,1)S(1)}, bf16[64,20,10]{2,0,1:T(8,128)(2,1)S(1)}, u32[]{:S(2)}, u32[]{:S(2)}) collective-permute-start(bf16[64,20,10]{2,0,1:T(8,128)(2,1)S(1)} %slice.66), channel_id=1, source_target_pairs={{0,1},{1,0},{2,3},{3,2},{4,5},{5,4},{6,7},{7,6},{8,9},{9,8},{10,11... | collective-permute-start | bytes 76808 | tf_op jit(solution)/shard_map/ppermute | solution.py:22
  319.8 6.1 copy-start.14
  389.9 10.0 copy-start.6
  399.9 8.2 copy-start.18
  473.1 13.2 copy-start.13
  541.8 23.6 %collective-permute-start = (bf16[64,10,720]{2,0,1:T(8,128)(2,1)S(1)}, bf16[64,10,720]{2,0,1:T(8,128)(2,1)S(1)}, u32[]{:S(2)}, u32[]{:S(2)}) collective-permute-start(bf16[64,10,720]{2,0,1:T(8,128)(2,1)S(1)} %copy.397), channel_id=1, source_target_pairs={{0,30},{2,0},{4,2},{6,4},{8,6},{10,8},{12,10},{14,12},{16,14},{18,... | collective-permute-start | bytes 2764808 | tf_op jit(solution)/shard_map/ppermute | solution.py:22
  572.6 4.5 collective-permute-start.1
  617.2 8.0 copy-start.15
  632.8 25.5 %slice-start = ((s8[4718592]{0:T(1024)(128)(4,1)}), s8[524288]{0:T(1024)(128)(4,1)S(1)}, s32[]{:S(2)}) async-start(s8[4718592]{0:T(1024)(128)(4,1)} %bitcast.158), calls=%async_computation.2 | async-start | bytes 1048576
  644.5 13.8 %slice-start.1 = ((s8[4718592]{0:T(1024)(128)(4,1)}), s8[4194304]{0:T(1024)(128)(4,1)S(1)}, s32[]{:S(2)}) async-start(s8[4718592]{0:T(1024)(128)(4,1)} %bitcast.158), calls=%async_computation.3 | async-start | bytes 8388608
  713.6 20.6 %collective-permute-start.4 = (bf16[64,10,720]{2,0,1:T(8,128)(2,1)S(1)}, bf16[64,10,720]{2,0,1:T(8,128)(2,1)S(1)}, u32[]{:S(2)}, u32[]{:S(2)}) collective-permute-start(bf16[64,10,720]{2,0,1:T(8,128)(2,1)S(1)} %copy.413), channel_id=1, source_target_pairs={{0,2},{2,4},{4,6},{6,8},{8,10},{10,12},{12,14},{14,16},{16,18},{18... | collective-permute-start | bytes 2764808 | tf_op jit(solution)/shard_map/ppermute | solution.py:22
  740.6 2.9 copy-start.4
  743.6 15.2 %collective-permute-start.5 = (bf16[64,20,10]{0,2,1:T(8,128)(2,1)S(1)}, bf16[64,20,10]{0,2,1:T(8,128)(2,1)S(1)}, u32[]{:S(2)}, u32[]{:S(2)}) collective-permute-start(bf16[64,20,10]{0,2,1:T(8,128)(2,1)S(1)} %slice.87), channel_id=1, source_target_pairs={{0,1},{1,0},{2,3},{3,2},{4,5},{5,4},{6,7},{7,6},{8,9},{9,8},{10,11... | collective-permute-start | bytes 76808 | tf_op jit(solution)/shard_map/ppermute | solution.py:22
  767.8 2.9 copy-start.3
  771.8 22.0 %collective-permute-start.6 = (bf16[64,10,720]{2,0,1:T(8,128)(2,1)S(1)}, bf16[64,10,720]{2,0,1:T(8,128)(2,1)S(1)}, u32[]{:S(2)}, u32[]{:S(2)}) collective-permute-start(bf16[64,10,720]{2,0,1:T(8,128)(2,1)S(1)} %copy.417), channel_id=1, source_target_pairs={{0,30},{2,0},{4,2},{6,4},{8,6},{10,8},{12,10},{14,12},{16,14},{18,... | collective-permute-start | bytes 2764808 | tf_op jit(solution)/shard_map/ppermute | solution.py:22
  801.2 4.5 collective-permute-start.7
  861.3 28.6 %slice-start.2 = ((s8[4718592]{0:T(1024)(128)(4,1)}), s8[524288]{0:T(1024)(128)(4,1)S(1)}, s32[]{:S(2)}) async-start(s8[4718592]{0:T(1024)(128)(4,1)} %bitcast.160), calls=%async_computation.4 | async-start | bytes 1048576
  873.0 16.9 %slice-start.3 = ((s8[4718592]{0:T(1024)(128)(4,1)}), s8[4194304]{0:T(1024)(128)(4,1)S(1)}, s32[]{:S(2)}) async-start(s8[4718592]{0:T(1024)(128)(4,1)} %bitcast.160), calls=%async_computation.5 | async-start | bytes 8388608
  945.2 20.0 %collective-permute-start.8 = (bf16[64,10,720]{2,0,1:T(8,128)(2,1)S(1)}, bf16[64,10,720]{2,0,1:T(8,128)(2,1)S(1)}, u32[]{:S(2)}, u32[]{:S(2)}) collective-permute-start(bf16[64,10,720]{2,0,1:T(8,128)(2,1)S(1)} %copy.427), channel_id=1, source_target_pairs={{0,2},{2,4},{4,6},{6,8},{8,10},{10,12},{12,14},{14,16},{16,18},{18... | collective-permute-start | bytes 2764808 | tf_op jit(solution)/shard_map/ppermute | solution.py:22
  971.9 3.0 copy-start.5
  975.0 13.3 collective-permute-start.9
  1061.9 28.8 %slice-start.4 = ((s8[4718592]{0:T(1024)(128)(4,1)}), s8[524288]{0:T(1024)(128)(4,1)S(1)}, s32[]{:S(2)}) async-start(s8[4718592]{0:T(1024)(128)(4,1)} %bitcast.171), calls=%async_computation.6 | async-start | bytes 1048576
  1073.7 17.0 %slice-start.5 = ((s8[4718592]{0:T(1024)(128)(4,1)}), s8[4194304]{0:T(1024)(128)(4,1)S(1)}, s32[]{:S(2)}) async-start(s8[4718592]{0:T(1024)(128)(4,1)} %bitcast.171), calls=%async_computation.7 | async-start | bytes 8388608
  1139.7 26.5 %all-to-all-start.1 = ((bf16[64,20,720]{2,1,0:T(8,128)(2,1)}), bf16[64,20,720]{2,1,0:T(8,128)(2,1)S(1)}, u32[]{:S(2)}, u32[]{:S(2)}) async-start(bf16[64,20,720]{2,1,0:T(8,128)(2,1)} %copy.439), calls=%async_computation.1 | async-start | bytes 4718592 | tf_op jit(solution)/shard_map/all_to_all | solution.py:217
  1143.5 3.9 copy-start.8
  1194.5 20.1 %copy-start.12 = (f32[640,721]{0,1:T(8,128)S(1)}, f32[640,721]{0,1:T(8,128)}, u32[]{:S(2)}) copy-start(f32[640,721]{0,1:T(8,128)} %copy.378) | copy-start | bytes 5537284
  1194.5 20.1 %copy-start.20 = (f32[721]{0:T(1024)S(1)}, f32[721]{0:T(1024)}, u32[]{:S(2)}) copy-start(f32[721]{0:T(1024)} %copy-done.19) | copy-start | bytes 8656
  1279.0 2.1 copy-start.2
  1347.2 11.3 copy-start.1
where the time goes:
time: 1370 us; the launch traced here: 1360 us
  local copies, waits for them, and re-layouts  640 us (47%)
  matrix products  411 us (30%)
  other arithmetic  113 us (8%)
  waiting for transfers between devices  101 us (7%)
  blocking collectives  60.6 us (4%)
  starting transfers between devices  20.4 us (1%)
    transpose x6, local copies, waits for them, and re-layouts, to_tokens(): return blocks.transpose(1, 3, 2, 4, 0).reshape(-1, win * win, depth)  94.8 us
    reshape x12, local copies, waits for them, and re-layouts, to_tokens(): return blocks.transpose(1, 3, 2, 4, 0).reshape(-1, win * win, depth)  91.4 us
    ppermute x10, waiting for transfers between devices, from_behind(): return lax.ppermute(value, axis, pairs)  86.1 us
    unnamed x72, local copies, waits for them, and re-layouts  81.3 us
    psum x1, blocking collectives, body(): current = lax.psum(current_part, ('grp', 'lat', 'lon'))  60.6 us
    dot_general x2, matrix products, attention_weights(): jnp.einsum('nthe,nshe->nhts', queries, keys_unit, preferred_element_type=...  60.5 us
    dot_general x2, matrix products, half_covariance(): jnp.dot(flat, cos_table, precision=triple_pass, preferred_element_type=jn...  51.2 us
    dot_general x2, matrix products, half_covariance(): jnp.dot(flat, sin_table, precision=triple_pass, preferred_element_type=jn...  49.9 us
  transfers between devices with their start and end apart: 12, of which 7 were waited for; matrix products, arithmetic and copies ran while one was open for 26% of the time, Pallas kernels for 0%

commit v1 on v0

v1 whole, which is shorter than its diff:
```python
import functools
import math

import jax
import jax.numpy as jnp
import numpy as np
from jax import lax
from jax.experimental import pallas as pl
from jax.experimental.pallas import tpu as pltpu
from jax.sharding import PartitionSpec as P

WIN = 10


precise = lax.Precision.HIGHEST


def as_sent(shard):
    return jax.tree.map(lambda a: a.astype(jnp.bfloat16) if a.dtype == jnp.float32 else a, shard)


def from_behind(value, axis, steps):
    count = lax.axis_size(axis)
    pairs = [(source, (source + steps) % count) for source in range(count)]
    return lax.ppermute(value, axis, pairs)


def wave_tables(lon_len, wave_count):
    place = np.arange(lon_len)[:, None]
    wave = np.arange(wave_count)[None, :]
    angle = (place * wave % lon_len) * (2.0 * math.pi / lon_len)
    pad = -wave_count % 128
    wide = ((0, 0), (0, pad))
    table = np.concatenate([np.pad(np.cos(angle), wide), np.pad(np.sin(angle), wide)], axis=1)
    table = table.astype(np.float32)
    coarse = table.astype(jnp.bfloat16)
    fine = (table - coarse.astype(np.float32)).astype(jnp.bfloat16)
    return coarse, fine


def split_pair(value):
    coarse = lax.reduce_precision(value, 8, 7)
    return coarse.astype(jnp.bfloat16), (value - coarse).astype(jnp.bfloat16)


def half_covariance(flat, scaled, tables):
    coarse, fine = tables
    wide = np.concatenate([coarse, coarse, fine], axis=0)
    tall = np.concatenate([coarse.T, coarse.T, fine.T], axis=0)
    if flat.dtype == jnp.bfloat16:
        left = jnp.concatenate([flat, flat], axis=1)
        wide = np.concatenate([coarse, fine], axis=0)
    else:
        big, small = split_pair(flat)
        left = jnp.concatenate([big, small, big], axis=1)
    parts = jnp.dot(left, jnp.asarray(wide), preferred_element_type=jnp.float32)
    big, small = split_pair(parts * scaled)
    left = jnp.concatenate([big, small, big], axis=1)
    return jnp.dot(left, jnp.asarray(tall), preferred_element_type=jnp.float32)


SPAN = 112
GROUP = 4


def dot(a, b):
    return jnp.dot(a, b, preferred_element_type=jnp.float32)


def lay_rows(source, place):
    for r in range(WIN):
        place[r] = source[r].astype(jnp.float32).T


def take_windows(place, at, tokens):
    width = WIN * GROUP
    for r in range(WIN):
        cells = place[r, pl.ds(pl.multiple_of(at * width, 8), width), :]
        for g in range(GROUP):
            tokens[g, r * WIN : (r + 1) * WIN, :] = cells[g * WIN : (g + 1) * WIN]
    return tokens[...].reshape(GROUP * SPAN, tokens.shape[2])


def put_windows(tokens, value, strip, at, place):
    width = WIN * GROUP
    tokens[...] = value.reshape(tokens.shape)
    for r in range(WIN):
        for g in range(GROUP):
            strip[r, g * WIN : (g + 1) * WIN, :] = tokens[g, r * WIN : (r + 1) * WIN, :]
    for r in range(WIN):
        place[r, pl.ds(pl.multiple_of(at * width, 8), width), :] = strip[r]


def unit_vectors(tokens, weight, ones):
    projected = dot(tokens, weight)
    squares = dot((projected * projected).astype(jnp.bfloat16), ones)
    return projected * lax.rsqrt(squares + 1e-06)


def window_probs(query, keys, head, g):
    rows = slice(g * SPAN, (g + 1) * SPAN)
    lanes = slice(head * 64, head * 64 + 64)
    scores = lax.dot_general(
        query[rows, lanes], keys[rows, lanes], (((1,), (1,)), ((), ())),
        preferred_element_type=jnp.float32,
    )
    inside = lax.broadcasted_iota(jnp.int32, scores.shape, 1) < WIN * WIN
    raised = jnp.where(inside, jnp.exp(scores), 0.0)
    return (raised / jnp.sum(raised, axis=1, keepdims=True)).astype(jnp.bfloat16)


def mix(probs, values, mixed, heads, across):
    for g in range(GROUP):
        rows = slice(g * SPAN, (g + 1) * SPAN)
        for h in range(heads):
            lanes = slice(h * 64, h * 64 + 64)
            mixed[rows, lanes] = lax.dot_general(
                probs(g, h), values[rows, lanes], (((across,), (0,)), ((), ())),
                preferred_element_type=jnp.float32,
            )
    return mixed[...].astype(jnp.bfloat16)


def single_kernel(heads, across, state_ref, field_ref, qw, kw, inw, outw, ones, scale,
                  out_ref, place_s, place_f, tok_s, tok_f, strip, mixed):
    tok_s[...] = jnp.zeros_like(tok_s)
    lay_rows(state_ref, place_s)
    lay_rows(field_ref, place_f)

    def body(at, carry):
        tok_f[...] = jnp.zeros_like(tok_f)
        state = take_windows(place_s, at, tok_s).astype(jnp.bfloat16)
        field = take_windows(place_f, at, tok_f)
        query = (unit_vectors(state, qw[...], ones[...]) * scale[...]).astype(jnp.bfloat16)
        keys = unit_vectors(state, kw[...], ones[...]).astype(jnp.bfloat16)
        values = dot(field.astype(jnp.bfloat16), inw[...]).astype(jnp.bfloat16)
        both = mix(lambda g, h: window_probs(query, keys, h, g), values, mixed, heads, across)
        put_windows(tok_f, field + dot(both, outw[...]), strip, at, place_f)
        return carry

    lax.fori_loop(0, place_f.shape[1] // (WIN * GROUP), body, 0)
    for r in range(WIN):
        out_ref[r] = place_f[r].T.astype(out_ref.dtype)


def double_kernel(heads, state_ref, field_ref, innov_ref, obs_ref, qw, kw, vw, ow, owt, vwt,
                  ones, scale, out_ref, sum_ref, place_s, place_f, place_i, place_o,
                  tok_s, tok_f, tok_i, tok_o, strip, mixed, held):
    tok_s[...] = jnp.zeros_like(tok_s)
    tok_i[...] = jnp.zeros_like(tok_i)
    tok_o[...] = jnp.zeros_like(tok_o)
    lay_rows(state_ref, place_s)
    lay_rows(field_ref, place_f)
    lay_rows(innov_ref, place_i)
    lay_rows(obs_ref, place_o)

    @pl.when(pl.program_id(0) == 0)
    def _():
        sum_ref[...] = jnp.zeros_like(sum_ref)

    def body(at, carry):
        tok_f[...] = jnp.zeros_like(tok_f)
        state = take_windows(place_s, at, tok_s).astype(jnp.bfloat16)
        field = take_windows(place_f, at, tok_f)
        query = (unit_vectors(state, qw[...], ones[...]) * scale[...]).astype(jnp.bfloat16)
        keys = unit_vectors(state, kw[...], ones[...]).astype(jnp.bfloat16)
        values = dot(field.astype(jnp.bfloat16), vw[...]).astype(jnp.bfloat16)

        def fresh(g, h):
            probs = window_probs(query, keys, h, g)
            held[g, h] = probs
            return probs

        both = mix(fresh, values, mixed, heads, 1)
        misfit = field + dot(both, ow[...]) - take_windows(place_i, at, tok_i)
        adjoint = take_windows(place_o, at, tok_o) * misfit
        sum_ref[...] += adjoint * misfit
        upward = dot(adjoint.astype(jnp.bfloat16), owt[...]).astype(jnp.bfloat16)
        back = mix(lambda g, h: held[g, h], upward, mixed, heads, 0)
        put_windows(tok_f, adjoint + dot(back, vwt[...]), strip, at, place_f)
        return carry

    lax.fori_loop(0, place_f.shape[1] // (WIN * GROUP), body, 0)
    for r in range(WIN):
        out_ref[r] = place_f[r].T


def call_windows(kernel, arrays, small, out_dtype, with_sum, heads):
    rows, depth, width = arrays[0].shape
    f32 = jnp.float32
    block = pl.BlockSpec((WIN, depth, width), lambda i: (i, 0, 0))
    whole = [pl.BlockSpec(s.shape, lambda i: (0, 0)) for s in small]
    out_shape = [jax.ShapeDtypeStruct((rows, depth, width), out_dtype)]
    out_specs = [block]
    if with_sum:
        out_shape.append(jax.ShapeDtypeStruct((GROUP * SPAN, depth), f32))
        out_specs.append(pl.BlockSpec((GROUP * SPAN, depth), lambda i: (0, 0)))
    scratch = [pltpu.VMEM((WIN, width, depth), f32) for _ in arrays]
    scratch += [pltpu.VMEM((GROUP, SPAN, depth), f32) for _ in arrays]
    scratch += [pltpu.VMEM((WIN, WIN * GROUP, depth), f32), pltpu.VMEM((GROUP * SPAN, heads * 64), f32)]
    if with_sum:
        scratch.append(pltpu.VMEM((GROUP, heads, SPAN, SPAN), jnp.bfloat16))
    return pl.pallas_call(
        kernel,
        grid=(rows // WIN,),
        in_specs=[block] * len(arrays) + whole,
        out_shape=out_shape,
        out_specs=out_specs,
        scratch_shapes=scratch,
        compiler_params=pltpu.CompilerParams(vmem_limit_bytes=56 * 2**20),
    )(*arrays, *small)


def roll_ahead(field, shifts):
    height, depth, width = field.shape
    below = from_behind(as_sent(field[:WIN]), ("grp", "lat"), -1).astype(field.dtype)
    moved = lax.dynamic_slice_in_dim(jnp.concatenate([field, below], axis=0), shifts[0], height, 0)
    beside = from_behind(as_sent(moved[:, :, :WIN]), "lon", -1).astype(field.dtype)
    return lax.dynamic_slice_in_dim(jnp.concatenate([moved, beside], axis=2), shifts[1], width, 2)


def roll_behind(field, shifts):
    height, depth, width = field.shape
    above = from_behind(as_sent(field[height - WIN :]), ("grp", "lat"), 1).astype(field.dtype)
    moved = lax.dynamic_slice_in_dim(
        jnp.concatenate([above, field], axis=0), WIN - shifts[0], height, 0
    )
    beside = from_behind(as_sent(moved[:, :, width - WIN :]), "lon", 1).astype(field.dtype)
    return lax.dynamic_slice_in_dim(
        jnp.concatenate([beside, moved], axis=2), WIN - shifts[1], width, 2
    )


def body(
    control,
    spectra,
    band_starts,
    band_spectrum,
    shifts,
    traj_start,
    traj_next,
    query_weight,
    key_weight,
    value_weight,
    out_weight,
    head_scale,
    innov_one,
    innov_two,
    obs_weight_one,
    obs_weight_two,
    grad_prev,
    dir_prev,
):
    fields_here, row_count, lon_len = control.shape
    spec_count, wave_count = (spectra.shape[0], spectra.shape[2])
    first_row = lax.axis_index(("grp", "lat")) * row_count
    global_rows = first_row + jnp.arange(row_count, dtype=jnp.int32)
    band_of_row = (
        jnp.sum((band_starts[None, :] <= global_rows[:, None]).astype(jnp.int32), axis=1) - 1
    )
    band_hits = band_of_row[:, None] == jnp.arange(band_starts.shape[0], dtype=jnp.int32)[None, :]
    spec_of_row = jnp.sum(jnp.where(band_hits, band_spectrum[None, :], 0), axis=1)
    selector = (spec_of_row[:, None] == jnp.arange(spec_count, dtype=jnp.int32)[None, :]).astype(
        jnp.float32
    )
    row_spec = jnp.einsum(
        "rs,sfk->rfk", selector, spectra, precision=precise, preferred_element_type=jnp.float32
    )
    tables = wave_tables(lon_len, wave_count)
    wave = np.arange(wave_count)
    weight = np.where((wave == 0) | (wave == lon_len // 2), 1.0, 2.0).astype(np.float32) / lon_len
    padded = jnp.pad(row_spec * weight, ((0, 0), (0, 0), (0, -wave_count % 128)))
    scaled = jnp.concatenate([padded, padded], axis=2).reshape(row_count * fields_here, -1)
    by_row = lambda a: jnp.transpose(a, (1, 0, 2))
    heads = head_scale.shape[0]
    inner = query_weight.shape[1]
    scale = jnp.repeat(head_scale, inner // heads)[None, :]
    ones = jnp.asarray(np.kron(np.eye(heads), np.ones((64, 64))), jnp.bfloat16)
    next_state = roll_ahead(by_row(traj_next), shifts)
    innov_next = roll_ahead(by_row(innov_two), shifts)
    obs_next = roll_ahead(by_row(obs_weight_two), shifts)
    start_state = by_row(traj_start)
    prior_part = jnp.sum(control * control)
    previous_part = jnp.sum(grad_prev * grad_prev)
    control_rows = by_row(control)
    start_cycle = half_covariance(control_rows.reshape(-1, lon_len), scaled, tables)
    start_cycle = start_cycle.astype(jnp.bfloat16).reshape(row_count, fields_here, lon_len)
    increment_start = lax.all_to_all(start_cycle, "lon", split_axis=2, concat_axis=1, tiled=True)
    forward = (query_weight, key_weight, value_weight, out_weight, ones, scale)
    backward = (query_weight, key_weight, out_weight.T, value_weight.T, ones, scale)
    increment_one = call_windows(
        functools.partial(single_kernel, heads, 1),
        [start_state, increment_start], forward, jnp.float32, False, heads,
    )[0]
    carried, misfit_cells = call_windows(
        functools.partial(double_kernel, heads),
        [next_state, roll_ahead(increment_one, shifts), innov_next, obs_next],
        (query_weight, key_weight, value_weight, out_weight, out_weight.T, value_weight.T, ones, scale),
        jnp.float32, True, heads,
    )
    misfit_one = increment_one - by_row(innov_one)
    adjoint_own = by_row(obs_weight_one) * misfit_one
    misfit_part = jnp.sum(adjoint_own * misfit_one) + jnp.sum(misfit_cells)
    prior, previous, misfit = lax.psum(
        (prior_part, previous_part, misfit_part), ("grp", "lat", "lon")
    )
    adjoint_one = roll_behind(carried, shifts) + adjoint_own
    adjoint_start = call_windows(
        functools.partial(single_kernel, heads, 0),
        [start_state, adjoint_one], backward, jnp.bfloat16, False, heads,
    )[0]
    back_cycle = lax.all_to_all(adjoint_start, "lon", split_axis=1, concat_axis=2, tiled=True)
    smoothed = half_covariance(back_cycle.reshape(-1, lon_len), scaled, tables)
    gradient = control + by_row(smoothed.reshape(row_count, fields_here, lon_len))
    current = lax.psum(jnp.sum(gradient * gradient), ("grp", "lat", "lon"))
    elements = fields_here * row_count * lon_len * lax.axis_size(("grp", "lat", "lon"))
    cost_value = 0.5 * (prior + misfit) / elements
    direction = -gradient + current / previous * dir_prev
    return (gradient, direction, cost_value)


def solution(mesh):
    in_specs = (
        P("lon", ("grp", "lat"), None),
        P(None, "lon", None),
        P(),
        P(),
        P(),
        P(None, ("grp", "lat"), "lon"),
        P(None, ("grp", "lat"), "lon"),
        P(),
        P(),
        P(),
        P(),
        P(),
        P(None, ("grp", "lat"), "lon"),
        P(None, ("grp", "lat"), "lon"),
        P(None, ("grp", "lat"), "lon"),
        P(None, ("grp", "lat"), "lon"),
        P("lon", ("grp", "lat"), None),
        P("lon", ("grp", "lat"), None),
    )
    out_specs = (P("lon", ("grp", "lat"), None), P("lon", ("grp", "lat"), None), P())
    return jax.shard_map(body, mesh=mesh, in_specs=in_specs, out_specs=out_specs, check_vma=False)
```

time: 1370 us -> 658 us (0.48)
  local copies, waits for them, and re-layouts: 640 us -> 95.2 us
  matrix products: 411 us -> 58.5 us
  Pallas kernels: 0 us -> 290 us
  other arithmetic: 113 us -> 54.6 us
  waiting for transfers between devices: 101 us -> 60.8 us
    dot_general x27 -> x12, matrix products: 411 us -> 58.5 us  [the longest x5 27.9 us: half_covariance(): parts = jnp.dot(left, jnp.asarray(wide), preferred_element_type=jnp.float32)]
    pallas_call x0 -> x3, Pallas kernels: none -> 290 us  [call_windows(): pl.pallas_call(kernel, grid=(rows // WIN,), in_specs=[block] * len(arrays...]
    reshape x28 -> x3, local copies, waits for them, and re-layouts: 214 us -> 19.5 us  [the longest x1 8.93 us: body(): start_cycle.astype(jnp.bfloat16).reshape(row_count, fields_here, lon_len)]
    convert_element_type x19 -> x1, local copies, waits for them, and re-layouts: 148 us -> 2.65 us  [body(): start_cycle.astype(jnp.bfloat16).reshape(row_count, fields_here, lon_len)]
    transpose x9 -> x0, local copies, waits for them, and re-layouts: 144 us -> none  [the longest x6 94.8 us: to_tokens(): return blocks.transpose(1, 3, 2, 4, 0).reshape(-1, win * win, depth)]
    unnamed x72 -> x62, local copies, waits for them, and re-layouts: 81.3 us -> 28.1 us
    ppermute x10, waiting for transfers between devices: 86.1 us -> 34.8 us  [from_behind(): return lax.ppermute(value, axis, pairs)]
    add x4 -> x0, local copies, waits for them, and re-layouts: 30.7 us -> none  [the longest x2 16.8 us: window_forward(): tokens + jnp.einsum('ntd,dc->ntc', mixed, out_weight, preferred_element_t...]
  transfers between devices with their start and end apart: 12 -> 12, of which waited for: 7 -> 7; matrix products, arithmetic and copies ran while one was open for 26% -> 9% of each run, Pallas kernels for 0% -> 13%
where the time goes in v1:
time: 658 us; the launch traced here: 652 us
  Pallas kernels  290 us (44%)
  local copies, waits for them, and re-layouts  95.2 us (14%)
  blocking collectives  63 us (10%)
  waiting for transfers between devices  60.8 us (9%)
  matrix products  58.5 us (9%)
  other arithmetic  54.6 us (8%)
  starting transfers between devices  17.2 us (3%)
  between operations  12.8 us (2%)
    pallas_call x3, Pallas kernels, call_windows(): pl.pallas_call(kernel, grid=(rows // WIN,), in_specs=[block] * len(arrays...  290 us
    psum x1, blocking collectives, body(): current = lax.psum(jnp.sum(gradient * gradient), ('grp', 'lat', 'lon'))  63 us
    ppermute x10, waiting for transfers between devices, from_behind(): return lax.ppermute(value, axis, pairs)  34.8 us
    unnamed x62, local copies, waits for them, and re-layouts  28.1 us
    dot_general x5, matrix products, half_covariance(): parts = jnp.dot(left, jnp.asarray(wide), preferred_element_type=jnp.float32)  27.9 us
    dot_general x6, matrix products, half_covariance(): return jnp.dot(left, jnp.asarray(tall), preferred_element_type=jnp.float32)  27.4 us
    all_to_all x1, waiting for transfers between devices, body(): lax.all_to_all(adjoint_start, 'lon', split_axis=1, concat_axis=2, tiled=T...  18.5 us
    all_to_all x2, local copies, waits for them, and re-layouts, body(): lax.all_to_all(start_cycle, 'lon', split_axis=2, concat_axis=1, tiled=True)  16.4 us
  transfers between devices with their start and end apart: 12, of which 7 were waited for; matrix products, arithmetic and copies ran while one was open for 9% of the time, Pallas kernels for 13%

profile of v1, /device:TPU:12, one launch (start us, length us, event | category | flops | bytes accessed | tf_op | source)
XLA Modules:
  0.0 652.0 jit_solution(1618283284078419608)
XLA Ops:
  0.7 1.0 convert_reduce_fusion
  1.7 0.8 select_reduce_fusion
  2.5 3.3 fusion.16
  6.7 4.2 copy.63
  10.9 5.7 copy.64
  16.6 2.8 reduce-precision_convert_fusion.2
  20.0 5.9 fusion.25
  25.8 5.8 fusion.26
  31.6 7.4 %fusion.8 = f32[640,1536]{0,1:T(8,128)S(1)} fusion(f32[640,1536]{0,1:T(8,128)S(1)} %copy-done.9, f32[640,1536]{0,1:T(8,128)} %fusion.26, f32[1536,640]{1,0:T(8,128)} %fusion.25, bf16[1440,1536]{1,0:T(8,128)(2,1)S(1)} %bitcast.97, bf16[640,1440]{1,0:T(8,128)(2,1)S(1)} %get-tuple-element.15), kind=kOutput, calls=%fused_computation.30 | convolution fusion | flops 2834104320 | bytes 21995520 | tf_op jit(solution)/shard_map/dot_general | solution.py:56
  39.0 4.0 fusion.14
  43.0 4.0 fusion.19
  47.1 5.3 add_convert_fusion
  52.4 2.6 copy.65
  55.0 8.9 %copy.66 = bf16[20,32,1440]{1,0,2:T(8,128)(2,1)} copy(bf16[20,32,1440]{2,1,0:T(8,128)(2,1)S(1)} %bitcast.74) | data formatting | bytes 3686400 | tf_op jit(solution)/shard_map/reshape | solution.py:287
  64.0 12.8 %reshape.39 = bf16[2,2,230400]{2,1,0:T(2,128)(2,1)} reshape(bf16[1440,20,32]{2,1,0:T(8,128)(2,1)} %bitcast.66) | data formatting | bytes 3686400
  76.8 3.9 all-to-all-start
  80.7 2.8 slice.94
  84.0 2.6 slice.95
  86.6 1.4 collective-permute-start.4
  88.0 1.0 slice.75
  95.6 7.4 %all-to-all-done = bf16[2,2,230400]{2,1,0:T(2,128)(2,1)S(1)} async-done(((bf16[2,2,230400]{2,1,0:T(2,128)(2,1)}), bf16[2,2,230400]{2,1,0:T(2,128)(2,1)S(1)}, u32[]{:S(2)}, u32[]{:S(2)}) %all-to-all-start) | async-done | bytes 1843232 | tf_op jit(solution)/shard_map/all_to_all | solution.py:288
  103.0 11.4 %reshape.40 = bf16[1440,20,32]{2,1,0:T(8,128)(2,1)} reshape(bf16[2,2,230400]{2,1,0:T(2,128)(2,1)S(1)} %all-to-all-done) | data formatting | bytes 3686400
  114.4 14.7 %copy.76 = bf16[20,32,2,720]{3,2,1,0:T(2,128)(2,1)S(1)} copy(bf16[20,32,2,720]{1,0,3,2:T(8,128)(2,1)} %bitcast.67) | data formatting | bytes 3686400 | tf_op jit(solution)/shard_map/all_to_all | solution.py:288
  129.1 1.7 copy.68
  130.8 87.7 %shard_map.247 = f32[20,64,720]{2,1,0:T(8,128)} custom-call(bf16[20,64,720]{2,1,0:T(8,128)(2,1)} %bitcast.76, bf16[20,64,720]{2,1,0:T(8,128)(2,1)} %bitcast.75, bf16[64,256]{1,0:T(8,128)(2,1)} %qw.5, bf16[64,256]{1,0:T(8,128)(2,1)} %kw.5, bf16[64,256]{1,0:T(8,128)(2,1)} %vw.1, bf16[256,64]{1,0:T(8,128)(2,1)} %copy.69.outw.ow, ...), custom_call_target="tpu_custom_call" | custom-call | tf_op jit(solution)/shard_map/pallas_call | solution.py:203
  218.6 1.8 slice.96
  220.4 1.0 collective-permute-start.2
  221.3 1.4 convert_element_type.69
  222.7 0.7 fusion.4
  223.9 1.4 convert_element_type.67
  225.4 0.7 fusion.5
  226.2 1.8 collective-permute-start.5
  229.4 4.9 collective-permute-done.7
  234.3 7.0 %collective-permute-done.5 = bf16[20,64,10]{2,1,0:T(8,128)(2,1)S(1)} collective-permute-done((bf16[20,64,10]{2,1,0:T(8,128)(2,1)S(1)}, bf16[20,64,10]{2,1,0:T(8,128)(2,1)S(1)}, u32[]{:S(2)}, u32[]{:S(2)}) %collective-permute-start.5) | collective-permute-done | bytes 25632 | tf_op jit(solution)/shard_map/ppermute | solution.py:25
  241.4 4.0 dynamic-slice_maximum_fusion.1.obs_ref
  245.4 4.0 dynamic-slice_maximum_fusion.2.innov_ref
  249.6 0.7 fusion.6
  250.7 3.1 dynamic-slice_maximum_fusion.4.state_ref
  253.9 3.6 collective-permute-done.3
  257.6 4.1 dynamic-slice_maximum_fusion.3.field_ref
  261.7 119.4 %shard_map.248 = (f32[20,64,720]{2,1,0:T(8,128)}, f32[448,64]{1,0:T(8,128)}) custom-call(bf16[20,64,720]{2,1,0:T(8,128)(2,1)} %dynamic-slice_maximum_fusion.4.state_ref, f32[20,64,720]{2,1,0:T(8,128)} %dynamic-slice_maximum_fusion.3.field_ref, f32[20,64,720]{2,1,0:T(8,128)} %dynamic-slice_maximum_fusion.2.innov_ref, ...), custom_call_target="tpu_custom_call" | custom-call | tf_op jit(solution)/shard_map/pallas_call | solution.py:203
  381.2 1.6 slice.93
  382.8 2.5 collective-permute-start.8
  386.6 14.4 %collective-permute-done.8 = bf16[10,64,720]{2,1,0:T(8,128)(2,1)S(1)} collective-permute-done((bf16[10,64,720]{2,1,0:T(8,128)(2,1)S(1)}, bf16[10,64,720]{2,1,0:T(8,128)(2,1)S(1)}, u32[]{:S(2)}, u32[]{:S(2)}) %collective-permute-start.8) | collective-permute-done | bytes 921632 | tf_op jit(solution)/shard_map/ppermute | solution.py:25
  401.2 2.0 fusion.3
  403.3 1.8 copy-done.3
  405.3 1.0 collective-permute-start.9
  407.5 4.9 collective-permute-done.9
  412.5 9.9 %multiply_reduce_fusion = (f32[]{:T(128)}, f32[20,64,720]{2,1,0:T(8,128)}) fusion(f32[64,20,720]{2,0,1:T(8,128)} %param.38, f32[20,64,720]{2,1,0:T(8,128)} %shard_map.247, f32[64,20,720]{2,0,1:T(8,128)} %param.36, s32[]{:T(128)S(6)} %select_n.26, f32[20,64,720]{2,1,0:T(8,128)} %copy-done.3, f32[20,64,10]{2,1,0:T(8,128)S(1)} %convert_element_type.72), kind=kLoop, calls=%fused_computation.33 | loop fusion | flops 5529599 | bytes 18483208 | tf_op jit(solution)/shard_map/reduce_sum | solution.py:303
  422.4 82.7 %shard_map.249 = bf16[20,64,720]{2,1,0:T(8,128)(2,1)} custom-call(bf16[20,64,720]{2,1,0:T(8,128)(2,1)} %bitcast.77, f32[20,64,720]{2,1,0:T(8,128)} %get-tuple-element.13.field_ref, bf16[64,256]{1,0:T(8,128)(2,1)} %qw.5, bf16[64,256]{1,0:T(8,128)(2,1)} %kw.5, bf16[64,256]{1,0:T(8,128)(2,1)} %bitcast.87, bf16[256,64]{1,0:T(8,128)(2,1)} %bitcast.85, ...), custom_call_target="tpu_custom_call" | custom-call | tf_op jit(solution)/shard_map/pallas_call | solution.py:203
  505.1 4.1 copy.72
  509.2 3.8 all-to-all-start.1
  514.9 18.5 %all-to-all-done.1 = bf16[20,64,720]{2,0,1:T(8,128)(2,1)S(1)} async-done(((bf16[20,64,720]{2,0,1:T(8,128)(2,1)}), bf16[20,64,720]{2,0,1:T(8,128)(2,1)S(1)}, u32[]{:S(2)}, u32[]{:S(2)}) %all-to-all-start.1) | async-done | bytes 1843232 | tf_op jit(solution)/shard_map/all_to_all | solution.py:312
  533.5 3.3 copy.82
  536.8 4.8 reshape.36
  541.6 5.6 fusion.27
  547.3 3.3 add_multiply_fusion
  550.6 3.9 fusion.12
  554.6 3.9 fusion.20
  558.6 6.2 add_add_fusion
  564.7 5.2 copy.74
  569.9 8.7 %multiply_reduce_fusion.3 = (f32[]{:T(128)}, f32[32,20,1440]{2,0,1:T(8,128)}, f32[]{:T(128)}, f32[]{:T(128)}) fusion(f32[32,20,1440]{2,0,1:T(8,128)} %param.24, f32[32,20,1440]{2,0,1:T(8,128)} %bitcast.70, f32[32,20,1440]{2,0,1:T(8,128)} %param.40), kind=kLoop, calls=%fused_computation.37 | loop fusion | flops 6451197 | bytes 14745612 | tf_op jit(solution)/shard_map/reduce_sum | solution.py:315
  579.2 63.0 %all-reduce.1 = (f32[]{:T(128)}, f32[]{:T(128)}, f32[]{:T(128)}) all-reduce(f32[]{:T(128)} %get-tuple-element.10, f32[]{:T(128)} %get-tuple-element.19, f32[]{:T(128)S(6)} %add.74), channel_id=1, replica_groups=mesh['grp'=2,'lat'=8,'lon'=2] {'grp','lat','lon'}, use_global_device_ids=true, to_apply=%region_3.4 | all-reduce | flops 3 | bytes 24 | tf_op jit(solution)/shard_map/psum | solution.py:315
  644.2 6.4 multiply_add_fusion
  (96 shorter events, 8.5 us)
Async XLA Ops:
  0.6 1.9 copy-start
  10.9 8.6 %slice-start.12 = ((s8[4423680]{0:T(1024)(128)(4,1)}), s8[229376]{0:T(1024)(128)(4,1)S(1)}, s32[]{:S(2)}) async-start(s8[4423680]{0:T(1024)(128)(4,1)} %bitcast.100), calls=%async_computation.14 | async-start | bytes 458752
  16.6 3.4 slice-start.13
  20.0 11.6 %slice-start.8 = ((s8[4423680]{0:T(1024)(128)(4,1)}), s8[4194304]{0:T(1024)(128)(4,1)S(1)}, s32[]{:S(2)}) async-start(s8[4423680]{0:T(1024)(128)(4,1)} %bitcast.96), calls=%async_computation.10 | async-start | bytes 8388608
  25.8 5.8 copy-start.9
  25.8 5.8 slice-start.9
  25.8 13.2 %slice-start.4 = ((s8[4718592]{0:T(1024)(128)(4,1)}), s8[4194304]{0:T(1024)(128)(4,1)S(1)}, s32[]{:S(2)}) async-start(s8[4718592]{0:T(1024)(128)(4,1)} %bitcast.92), calls=%async_computation.6 | async-start | bytes 8388608
  31.6 7.4 %slice-start.5 = ((s8[4718592]{0:T(1024)(128)(4,1)}), s8[524288]{0:T(1024)(128)(4,1)S(1)}, s32[]{:S(2)}) async-start(s8[4718592]{0:T(1024)(128)(4,1)} %bitcast.92), calls=%async_computation.7 | async-start | bytes 1048576
  31.6 15.4 %slice-start = ((s8[4718592]{0:T(1024)(128)(4,1)}), s8[4194304]{0:T(1024)(128)(4,1)S(1)}, s32[]{:S(2)}) async-start(s8[4718592]{0:T(1024)(128)(4,1)} %bitcast.88), calls=%async_computation.2 | async-start | bytes 8388608
  39.0 8.0 %slice-start.1 = ((s8[4718592]{0:T(1024)(128)(4,1)}), s8[524288]{0:T(1024)(128)(4,1)S(1)}, s32[]{:S(2)}) async-start(s8[4718592]{0:T(1024)(128)(4,1)} %bitcast.88), calls=%async_computation.3 | async-start | bytes 1048576
  76.8 12.2 %copy-start.14 = (f32[4]{0:T(128)S(1)}, f32[4]{0:T(128)}, u32[]{:S(2)}) copy-start(f32[4]{0:T(128)} %param.35) | copy-start | bytes 52
  76.8 13.0 %copy-start.11 = (bf16[256,64]{0,1:T(8,128)(2,1)S(1)}, bf16[256,64]{0,1:T(8,128)(2,1)}, u32[]{:S(2)}) copy-start(bf16[256,64]{0,1:T(8,128)(2,1)} %param.34) | copy-start | bytes 98308
  76.8 13.7 %copy-start.13 = (s32[2]{0:T(128)S(1)}, s32[2]{0:T(128)}, u32[]{:S(2)}) copy-start(s32[2]{0:T(128)} %param.28) | copy-start | bytes 28
  76.8 26.2 %all-to-all-start = ((bf16[2,2,230400]{2,1,0:T(2,128)(2,1)}), bf16[2,2,230400]{2,1,0:T(2,128)(2,1)S(1)}, u32[]{:S(2)}, u32[]{:S(2)}) async-start(bf16[2,2,230400]{2,1,0:T(2,128)(2,1)} %reshape.39), calls=%async_computation | async-start | bytes 3686400 | tf_op jit(solution)/shard_map/all_to_all | solution.py:288
  80.6 7.3 %copy-start.7 = (bf16[64,20,720]{2,0,1:T(8,128)(2,1)S(1)}, bf16[64,20,720]{2,0,1:T(8,128)(2,1)}, u32[]{:S(2)}) copy-start(bf16[64,20,720]{2,0,1:T(8,128)(2,1)} %param.30) | copy-start | bytes 5529604
  80.6 12.9 %copy-start.10 = (bf16[64,256]{1,0:T(8,128)(2,1)S(1)}, bf16[64,256]{1,0:T(8,128)(2,1)}, u32[]{:S(2)}) copy-start(bf16[64,256]{1,0:T(8,128)(2,1)} %vw.1) | copy-start | bytes 98308
  83.5 137.9 %collective-permute-start.6 = (bf16[10,64,720]{2,1,0:T(8,128)(2,1)}, bf16[10,64,720]{2,1,0:T(8,128)(2,1)}, u32[]{:S(2)}, u32[]{:S(2)}) collective-permute-start(bf16[10,64,720]{2,1,0:T(8,128)(2,1)} %slice.94), channel_id=1, source_target_pairs={{0,30},{2,0},{4,2},{6,4},{8,6},{10,8},{12,10},{14,12},{16,14},{18,... | collective-permute-start | bytes 2764808 | tf_op jit(solution)/shard_map/ppermute | solution.py:25
  86.6 137.3 %collective-permute-start.4 = (bf16[10,64,720]{2,1,0:T(8,128)(2,1)}, bf16[10,64,720]{2,1,0:T(8,128)(2,1)}, u32[]{:S(2)}, u32[]{:S(2)}) collective-permute-start(bf16[10,64,720]{2,1,0:T(8,128)(2,1)} %slice.95), channel_id=1, source_target_pairs={{0,30},{2,0},{4,2},{6,4},{8,6},{10,8},{12,10},{14,12},{16,14},{18,... | collective-permute-start | bytes 2764808 | tf_op jit(solution)/shard_map/ppermute | solution.py:25
  89.0 138.9 %collective-permute-start = (bf16[10,64,720]{2,1,0:T(8,128)(2,1)}, bf16[10,64,720]{2,1,0:T(8,128)(2,1)S(1)}, u32[]{:S(2)}, u32[]{:S(2)}) collective-permute-start(bf16[10,64,720]{2,1,0:T(8,128)(2,1)} %slice.75), channel_id=1, source_target_pairs={{0,30},{2,0},{4,2},{6,4},{8,6},{10,8},{12,10},{14,12},{16,14},{18,... | collective-permute-start | bytes 2764808 | tf_op jit(solution)/shard_map/ppermute | solution.py:25
  218.6 4.2 copy-start.5
  220.4 29.0 %collective-permute-start.2 = (bf16[10,64,720]{2,1,0:T(8,128)(2,1)S(1)}, bf16[10,64,720]{2,1,0:T(8,128)(2,1)S(1)}, u32[]{:S(2)}, u32[]{:S(2)}) collective-permute-start(bf16[10,64,720]{2,1,0:T(8,128)(2,1)S(1)} %slice.96), channel_id=1, source_target_pairs={{0,30},{2,0},{4,2},{6,4},{8,6},{10,8},{12,10},{14,12},{16,14},{18,... | collective-permute-start | bytes 2764808 | tf_op jit(solution)/shard_map/ppermute | solution.py:25
  222.7 2.6 copy-start.6
  223.6 10.7 %collective-permute-start.7 = (bf16[20,64,10]{2,1,0:T(8,128)(2,1)S(1)}, bf16[20,64,10]{2,1,0:T(8,128)(2,1)S(1)}, u32[]{:S(2)}, u32[]{:S(2)}) collective-permute-start(bf16[20,64,10]{2,1,0:T(8,128)(2,1)S(1)} %slice.98), channel_id=1, source_target_pairs={{0,1},{1,0},{2,3},{3,2},{4,5},{5,4},{6,7},{7,6},{8,9},{9,8},{10,11... | collective-permute-start | bytes 76808 | tf_op jit(solution)/shard_map/ppermute | solution.py:25
  225.3 2.6 copy-start.8
  226.2 15.1 %collective-permute-start.5 = (bf16[20,64,10]{2,1,0:T(8,128)(2,1)S(1)}, bf16[20,64,10]{2,1,0:T(8,128)(2,1)S(1)}, u32[]{:S(2)}, u32[]{:S(2)}) collective-permute-start(bf16[20,64,10]{2,1,0:T(8,128)(2,1)S(1)} %slice.99), channel_id=1, source_target_pairs={{0,1},{1,0},{2,3},{3,2},{4,5},{5,4},{6,7},{7,6},{8,9},{9,8},{10,11... | collective-permute-start | bytes 76808 | tf_op jit(solution)/shard_map/ppermute | solution.py:25
  228.6 22.1 %collective-permute-start.1 = (bf16[20,64,10]{2,1,0:T(8,128)(2,1)S(1)}, bf16[20,64,10]{2,1,0:T(8,128)(2,1)S(1)}, u32[]{:S(2)}, u32[]{:S(2)}) collective-permute-start(bf16[20,64,10]{2,1,0:T(8,128)(2,1)S(1)} %slice.76), channel_id=1, source_target_pairs={{0,1},{1,0},{2,3},{3,2},{4,5},{5,4},{6,7},{7,6},{8,9},{9,8},{10,11... | collective-permute-start | bytes 76808 | tf_op jit(solution)/shard_map/ppermute | solution.py:25
  245.3 4.2 copy-start.2
  250.4 7.1 %collective-permute-start.3 = (bf16[20,64,10]{2,1,0:T(8,128)(2,1)S(1)}, bf16[20,64,10]{2,1,0:T(8,128)(2,1)S(1)}, u32[]{:S(2)}, u32[]{:S(2)}) collective-permute-start(bf16[20,64,10]{2,1,0:T(8,128)(2,1)S(1)} %slice.100), channel_id=1, source_target_pairs={{0,1},{1,0},{2,3},{3,2},{4,5},{5,4},{6,7},{7,6},{8,9},{9,8},{10,11... | collective-permute-start | bytes 76808 | tf_op jit(solution)/shard_map/ppermute | solution.py:25
  382.8 18.2 %collective-permute-start.8 = (bf16[10,64,720]{2,1,0:T(8,128)(2,1)S(1)}, bf16[10,64,720]{2,1,0:T(8,128)(2,1)S(1)}, u32[]{:S(2)}, u32[]{:S(2)}) collective-permute-start(bf16[10,64,720]{2,1,0:T(8,128)(2,1)S(1)} %slice.93), channel_id=1, source_target_pairs={{0,2},{2,4},{4,6},{6,8},{8,10},{10,12},{12,14},{14,16},{16,18},{18... | collective-permute-start | bytes 2764808 | tf_op jit(solution)/shard_map/ppermute | solution.py:25
  403.2 1.9 copy-start.3
  405.3 7.1 %collective-permute-start.9 = (bf16[20,64,10]{2,1,0:T(8,128)(2,1)S(1)}, bf16[20,64,10]{2,1,0:T(8,128)(2,1)S(1)}, u32[]{:S(2)}, u32[]{:S(2)}) collective-permute-start(bf16[20,64,10]{2,1,0:T(8,128)(2,1)S(1)} %slice.97), channel_id=1, source_target_pairs={{0,1},{1,0},{2,3},{3,2},{4,5},{5,4},{6,7},{7,6},{8,9},{9,8},{10,11... | collective-permute-start | bytes 76808 | tf_op jit(solution)/shard_map/ppermute | solution.py:25
  505.1 7.9 %copy-start.12 = (f32[448,64]{1,0:T(8,128)S(1)}, f32[448,64]{1,0:T(8,128)}, u32[]{:S(2)}) copy-start(f32[448,64]{1,0:T(8,128)} %get-tuple-element.6) | copy-start | bytes 344068
  509.2 24.3 %all-to-all-start.1 = ((bf16[20,64,720]{2,0,1:T(8,128)(2,1)}), bf16[20,64,720]{2,0,1:T(8,128)(2,1)S(1)}, u32[]{:S(2)}, u32[]{:S(2)}) async-start(bf16[20,64,720]{2,0,1:T(8,128)(2,1)} %copy.72), calls=%async_computation.1 | async-start | bytes 4718592 | tf_op jit(solution)/shard_map/all_to_all | solution.py:312
  533.5 13.8 %slice-start.10 = ((s8[4423680]{0:T(1024)(128)(4,1)}), s8[229376]{0:T(1024)(128)(4,1)S(1)}, s32[]{:S(2)}) async-start(s8[4423680]{0:T(1024)(128)(4,1)} %bitcast.98), calls=%async_computation.12 | async-start | bytes 458752
  541.6 5.7 copy-start.4
  541.6 5.7 slice-start.11
  541.6 9.0 %slice-start.6 = ((s8[4718592]{0:T(1024)(128)(4,1)}), s8[4194304]{0:T(1024)(128)(4,1)S(1)}, s32[]{:S(2)}) async-start(s8[4718592]{0:T(1024)(128)(4,1)} %bitcast.94), calls=%async_computation.8 | async-start | bytes 8388608
  547.3 3.3 slice-start.7
  547.3 11.2 %slice-start.2 = ((s8[4718592]{0:T(1024)(128)(4,1)}), s8[4194304]{0:T(1024)(128)(4,1)S(1)}, s32[]{:S(2)}) async-start(s8[4718592]{0:T(1024)(128)(4,1)} %bitcast.90), calls=%async_computation.4 | async-start | bytes 8388608
  550.6 7.9 %slice-start.3 = ((s8[4718592]{0:T(1024)(128)(4,1)}), s8[524288]{0:T(1024)(128)(4,1)S(1)}, s32[]{:S(2)}) async-start(s8[4718592]{0:T(1024)(128)(4,1)} %bitcast.90), calls=%async_computation.5 | async-start | bytes 1048576
  644.2 6.4 copy-start.1

commit v2 on v1

--- a/solution.py
+++ b/solution.py
@@ -97,27 +97,38 @@
     return projected * lax.rsqrt(squares + 1e-06)
 
 
-def window_probs(query, keys, head, g):
+def lone_heads(query):
+    low = lax.broadcasted_iota(jnp.int32, query.shape, 1) % 128 < 64
+    return jnp.where(low, query, 0.0).astype(jnp.bfloat16), jnp.where(low, 0.0, query).astype(jnp.bfloat16)
+
+
+def window_probs(query, keys, head, g, across):
     rows = slice(g * SPAN, (g + 1) * SPAN)
-    lanes = slice(head * 64, head * 64 + 64)
+    lanes = slice(head // 2 * 128, head // 2 * 128 + 128)
+    pair = (query[head % 2][rows, lanes], keys[rows, lanes])
     scores = lax.dot_general(
-        query[rows, lanes], keys[rows, lanes], (((1,), (1,)), ((), ())),
+        pair[1 - across], pair[across], (((1,), (1,)), ((), ())),
         preferred_element_type=jnp.float32,
     )
-    inside = lax.broadcasted_iota(jnp.int32, scores.shape, 1) < WIN * WIN
+    inside = lax.broadcasted_iota(jnp.int32, scores.shape, across) < WIN * WIN
     raised = jnp.where(inside, jnp.exp(scores), 0.0)
-    return (raised / jnp.sum(raised, axis=1, keepdims=True)).astype(jnp.bfloat16)
+    return (raised * (1.0 / jnp.sum(raised, axis=across, keepdims=True))).astype(jnp.bfloat16)
 
 
 def mix(probs, values, mixed, heads, across):
+    low = lax.broadcasted_iota(jnp.int32, (SPAN, 128), 1) < 64
     for g in range(GROUP):
         rows = slice(g * SPAN, (g + 1) * SPAN)
-        for h in range(heads):
-            lanes = slice(h * 64, h * 64 + 64)
-            mixed[rows, lanes] = lax.dot_general(
-                probs(g, h), values[rows, lanes], (((across,), (0,)), ((), ())),
-                preferred_element_type=jnp.float32,
+        for h in range(0, heads, 2):
+            lanes = slice(h * 64, h * 64 + 128)
+            first, second = (
+                lax.dot_general(
+                    probs(g, h + k), values[rows, lanes], (((across,), (0,)), ((), ())),
+                    preferred_element_type=jnp.float32,
+                )
+                for k in range(2)
             )
+            mixed[rows, lanes] = jnp.where(low, first, second)
     return mixed[...].astype(jnp.bfloat16)
 
 
@@ -131,10 +142,10 @@
         tok_f[...] = jnp.zeros_like(tok_f)
         state = take_windows(place_s, at, tok_s).astype(jnp.bfloat16)
         field = take_windows(place_f, at, tok_f)
-        query = (unit_vectors(state, qw[...], ones[...]) * scale[...]).astype(jnp.bfloat16)
+        query = lone_heads(unit_vectors(state, qw[...], ones[...]) * scale[...])
         keys = unit_vectors(state, kw[...], ones[...]).astype(jnp.bfloat16)
         values = dot(field.astype(jnp.bfloat16), inw[...]).astype(jnp.bfloat16)
-        both = mix(lambda g, h: window_probs(query, keys, h, g), values, mixed, heads, across)
+        both = mix(lambda g, h: window_probs(query, keys, h, g, across), values, mixed, heads, 1)
         put_windows(tok_f, field + dot(both, outw[...]), strip, at, place_f)
         return carry
 
@@ -162,12 +173,12 @@
         tok_f[...] = jnp.zeros_like(tok_f)
         state = take_windows(place_s, at, tok_s).astype(jnp.bfloat16)
         field = take_windows(place_f, at, tok_f)
-        query = (unit_vectors(state, qw[...], ones[...]) * scale[...]).astype(jnp.bfloat16)
+        query = lone_heads(unit_vectors(state, qw[...], ones[...]) * scale[...])
         keys = unit_vectors(state, kw[...], ones[...]).astype(jnp.bfloat16)
         values = dot(field.astype(jnp.bfloat16), vw[...]).astype(jnp.bfloat16)
 
         def fresh(g, h):
-            probs = window_probs(query, keys, h, g)
+            probs = window_probs(query, keys, h, g, 1)
             held[g, h] = probs
             return probs
 
@@ -284,8 +295,12 @@
     previous_part = jnp.sum(grad_prev * grad_prev)
     control_rows = by_row(control)
     start_cycle = half_covariance(control_rows.reshape(-1, lon_len), scaled, tables)
-    start_cycle = start_cycle.astype(jnp.bfloat16).reshape(row_count, fields_here, lon_len)
-    increment_start = lax.all_to_all(start_cycle, "lon", split_axis=2, concat_axis=1, tiled=True)
+    owners = lax.axis_size("lon")
+    width = lon_len // owners
+    blocks = jnp.stack([start_cycle[:, n * width : (n + 1) * width] for n in range(owners)])
+    blocks = blocks.astype(jnp.bfloat16).reshape(owners, row_count, fields_here, width)
+    blocks = lax.all_to_all(blocks, "lon", split_axis=0, concat_axis=0, tiled=True)
+    increment_start = jnp.concatenate([blocks[n] for n in range(owners)], axis=1)
     forward = (query_weight, key_weight, value_weight, out_weight, ones, scale)
     backward = (query_weight, key_weight, out_weight.T, value_weight.T, ones, scale)
     increment_one = call_windows(

time: 658 us -> 543 us (0.83)
  Pallas kernels: 290 us -> 219 us
  local copies, waits for them, and re-layouts: 95.2 us -> 45.3 us
    pallas_call x3, Pallas kernels: 290 us -> 219 us  [call_windows(): pl.pallas_call(kernel, grid=(rows // WIN,), in_specs=[block] * len(arrays...]
    unnamed x62 -> x60, local copies, waits for them, and re-layouts: 28.1 us -> 3.97 us
    all_to_all x2 -> x0, local copies, waits for them, and re-layouts: 16.4 us -> none  [body(): lax.all_to_all(start_cycle, 'lon', split_axis=2, concat_axis=1, tiled=True)]
    reshape x1 -> x0, local copies, waits for them, and re-layouts: 8.93 us -> none  [body(): start_cycle.astype(jnp.bfloat16).reshape(row_count, fields_here, lon_len)]
  transfers between devices with their start and end apart: 12 -> 12, of which waited for: 7 -> 7; matrix products, arithmetic and copies ran while one was open for 9% -> 6% of each run, Pallas kernels for 13% -> 12%
where the time goes in v2:
time: 543 us; the launch traced here: 537 us
  Pallas kernels  219 us (40%)
  blocking collectives  63.1 us (12%)
  waiting for transfers between devices  61.9 us (11%)
  matrix products  60.7 us (11%)
  other arithmetic  57.8 us (11%)
  local copies, waits for them, and re-layouts  45.3 us (8%)
  starting transfers between devices  16.9 us (3%)
  between operations  12.8 us (2%)
    pallas_call x3, Pallas kernels, call_windows(): pl.pallas_call(kernel, grid=(rows // WIN,), in_specs=[block] * len(arrays...  219 us
    psum x1, blocking collectives, body(): current = lax.psum(jnp.sum(gradient * gradient), ('grp', 'lat', 'lon'))  63.1 us
    ppermute x10, waiting for transfers between devices, from_behind(): return lax.ppermute(value, axis, pairs)  34.8 us
    dot_general x6, matrix products, half_covariance(): return jnp.dot(left, jnp.asarray(tall), preferred_element_type=jnp.float32)  29.8 us
    dot_general x5, matrix products, half_covariance(): parts = jnp.dot(left, jnp.asarray(wide), preferred_element_type=jnp.float32)  27.6 us
    all_to_all x1, waiting for transfers between devices, body(): lax.all_to_all(adjoint_start, 'lon', split_axis=1, concat_axis=2, tiled=T...  18.5 us
    concatenate x4, other arithmetic, roll_ahead(): jnp.concatenate([moved, beside], axis=2)  15.5 us
  transfers between devices with their start and end apart: 12, of which 7 were waited for; matrix products, arithmetic and copies ran while one was open for 6% of the time, Pallas kernels for 12%

profile of v2, /device:TPU:12, one launch (start us, length us, event | category | flops | bytes accessed | tf_op | source)
XLA Modules:
  0.0 537.4 jit_solution(14957231962443592663)
XLA Ops:
  0.7 1.0 convert_reduce_fusion
  1.7 0.8 select_reduce_fusion
  2.5 3.3 fusion.16
  6.7 4.2 copy.63
  10.9 5.6 %copy.64 = f32[640,1536]{0,1:T(8,128)} copy(f32[640,1536]{1,0:T(8,128)} %bitcast.66) | data formatting | bytes 7864320 | tf_op jit(solution)/shard_map/reshape | solution.py:284
  16.5 2.8 reduce-precision_convert_fusion.2
  19.9 5.8 %fusion.26 = f32[1536,640]{1,0:T(8,128)} fusion(bf16[1440,1536]{1,0:T(8,128)(2,1)S(1)} %bitcast.98, bf16[640,1440]{1,0:T(8,128)(2,1)S(1)} %get-tuple-element.15), kind=kOutput, calls=%fused_computation.74 | convolution fusion | flops 2831155200 | bytes 10199040 | tf_op jit(solution)/shard_map/dot_general | solution.py:56
  25.8 5.8 %fusion.27 = f32[640,1536]{0,1:T(8,128)} fusion(bf16[640,1440]{1,0:T(8,128)(2,1)S(1)} %get-tuple-element.16, bf16[1440,1536]{1,0:T(8,128)(2,1)S(1)} %bitcast.98), kind=kOutput, calls=%fused_computation.75 | convolution fusion | flops 2831155200 | bytes 10199040 | tf_op jit(solution)/shard_map/dot_general | solution.py:56
  31.6 7.3 %fusion.8 = f32[640,1536]{0,1:T(8,128)S(1)} fusion(f32[640,1536]{0,1:T(8,128)S(1)} %copy-done.9, f32[640,1536]{0,1:T(8,128)} %fusion.27, f32[1536,640]{1,0:T(8,128)} %fusion.26, bf16[1440,1536]{1,0:T(8,128)(2,1)S(1)} %bitcast.94, bf16[640,1440]{1,0:T(8,128)(2,1)S(1)} %get-tuple-element.15), kind=kOutput, calls=%fused_computation.30 | convolution fusion | flops 2834104320 | bytes 21995520 | tf_op jit(solution)/shard_map/dot_general | solution.py:56
  38.9 4.0 fusion.14
  42.9 5.7 %fusion.19 = f32[640,1440]{0,1:T(8,128)} fusion(bf16[1536,1440]{1,0:T(8,128)(2,1)S(1)} %bitcast.90, f32[640,1536]{0,1:T(8,128)S(1)} %fusion.8), kind=kOutput, calls=%fused_computation.58 | convolution fusion | flops 2833121280 | bytes 12042240 | tf_op jit(solution)/shard_map/dot_general | solution.py:59
  48.7 6.0 %add_convert_fusion = bf16[640,1440]{0,1:T(8,128)(2,1)S(1)} fusion(f32[640,1440]{0,1:T(8,128)} %fusion.19, f32[640,1440]{0,1:T(8,128)S(1)} %fusion.14, bf16[1536,1440]{1,0:T(8,128)(2,1)S(1)} %bitcast.86, f32[640,1536]{0,1:T(8,128)S(1)} %fusion.8), kind=kOutput, calls=%fused_computation.39 | convolution fusion | flops 2835886080 | bytes 17571840 | tf_op jit(solution)/shard_map/dot_general | solution.py:59
  54.8 1.0 copy.65
  55.9 1.0 copy.66
  56.9 1.5 pad_maximum_fusion.1
  58.4 3.7 all-to-all-start
  62.2 2.8 slice.118
  65.4 2.6 slice.119
  68.0 1.4 collective-permute-start.4
  69.4 1.0 slice.93
  71.8 0.7 copy.67.outw.ow
  75.1 0.7 copy.68
  77.1 8.7 %all-to-all-done = bf16[2,20,32,720]{3,2,1,0:T(8,128)(2,1)S(1)} async-done(((bf16[2,20,32,720]{3,2,1,0:T(8,128)(2,1)}), bf16[2,20,32,720]{3,2,1,0:T(8,128)(2,1)S(1)}, u32[]{:S(2)}, u32[]{:S(2)}) %all-to-all-start) | async-done | bytes 1843232 | tf_op jit(solution)/shard_map/all_to_all | solution.py:302
  85.9 1.5 pad_maximum_fusion.2.field_ref
  87.5 66.4 %shard_map.247 = f32[20,64,720]{2,1,0:T(8,128)} custom-call(bf16[20,64,720]{2,1,0:T(8,128)(2,1)} %bitcast.71, bf16[20,64,720]{2,1,0:T(8,128)(2,1)} %pad_maximum_fusion.2.field_ref, bf16[64,256]{1,0:T(8,128)(2,1)} %qw.5, bf16[64,256]{1,0:T(8,128)(2,1)} %kw.5, bf16[64,256]{1,0:T(8,128)(2,1)} %vw.1, bf16[256,64]{1,0:T(8,128)(2,1)} %copy.67.outw.ow, ...), custom_call_target="tpu_custom_call" | custom-call | tf_op jit(solution)/shard_map/pallas_call | solution.py:214
  153.9 1.8 slice.120
  155.7 0.7 collective-permute-start.2
  156.4 1.4 convert_element_type.67
  157.8 0.7 fusion.4
  159.0 1.4 convert_element_type.65
  160.4 0.7 fusion.5
  161.2 1.8 collective-permute-start.5
  164.4 4.9 collective-permute-done.7
  169.4 7.0 %collective-permute-done.5 = bf16[20,64,10]{2,1,0:T(8,128)(2,1)S(1)} collective-permute-done((bf16[20,64,10]{2,1,0:T(8,128)(2,1)S(1)}, bf16[20,64,10]{2,1,0:T(8,128)(2,1)S(1)}, u32[]{:S(2)}, u32[]{:S(2)}) %collective-permute-start.5) | collective-permute-done | bytes 25632 | tf_op jit(solution)/shard_map/ppermute | solution.py:25
  176.4 4.0 dynamic-slice_maximum_fusion.1.obs_ref
  180.4 4.0 dynamic-slice_maximum_fusion.2.innov_ref
  184.6 0.7 fusion.6
  185.8 3.1 dynamic-slice_maximum_fusion.4.state_ref
  188.9 3.6 collective-permute-done.3
  192.6 4.4 dynamic-slice_maximum_fusion.3.field_ref
  197.0 92.1 %shard_map.248 = (f32[20,64,720]{2,1,0:T(8,128)}, f32[448,64]{1,0:T(8,128)}) custom-call(bf16[20,64,720]{2,1,0:T(8,128)(2,1)} %dynamic-slice_maximum_fusion.4.state_ref, f32[20,64,720]{2,1,0:T(8,128)} %dynamic-slice_maximum_fusion.3.field_ref, f32[20,64,720]{2,1,0:T(8,128)} %dynamic-slice_maximum_fusion.2.innov_ref, ...), custom_call_target="tpu_custom_call" | custom-call | tf_op jit(solution)/shard_map/pallas_call | solution.py:214
  289.1 1.6 slice.117
  290.8 2.5 collective-permute-start.8
  294.6 14.4 %collective-permute-done.8 = bf16[10,64,720]{2,1,0:T(8,128)(2,1)S(1)} collective-permute-done((bf16[10,64,720]{2,1,0:T(8,128)(2,1)S(1)}, bf16[10,64,720]{2,1,0:T(8,128)(2,1)S(1)}, u32[]{:S(2)}, u32[]{:S(2)}) %collective-permute-start.8) | collective-permute-done | bytes 921632 | tf_op jit(solution)/shard_map/ppermute | solution.py:25
  309.1 2.0 fusion.3
  311.2 1.9 copy-done.3
  313.2 1.0 collective-permute-start.9
  315.5 4.9 collective-permute-done.9
  320.4 9.9 %multiply_reduce_fusion = (f32[]{:T(128)}, f32[20,64,720]{2,1,0:T(8,128)}) fusion(f32[64,20,720]{2,0,1:T(8,128)} %param.38, f32[20,64,720]{2,1,0:T(8,128)} %shard_map.247, f32[64,20,720]{2,0,1:T(8,128)} %param.36, s32[]{:T(128)S(6)} %select_n.26, f32[20,64,720]{2,1,0:T(8,128)} %copy-done.3, f32[20,64,10]{2,1,0:T(8,128)S(1)} %convert_element_type.70), kind=kLoop, calls=%fused_computation.33 | loop fusion | flops 5529599 | bytes 18483208 | tf_op jit(solution)/shard_map/reduce_sum | solution.py:318
  330.3 60.4 %shard_map.249 = bf16[20,64,720]{2,1,0:T(8,128)(2,1)} custom-call(bf16[20,64,720]{2,1,0:T(8,128)(2,1)} %bitcast.72, f32[20,64,720]{2,1,0:T(8,128)} %get-tuple-element.13.field_ref, bf16[64,256]{1,0:T(8,128)(2,1)} %qw.5, bf16[64,256]{1,0:T(8,128)(2,1)} %kw.5, bf16[64,256]{1,0:T(8,128)(2,1)} %bitcast.84, bf16[256,64]{1,0:T(8,128)(2,1)} %bitcast.82, ...), custom_call_target="tpu_custom_call" | custom-call | tf_op jit(solution)/shard_map/pallas_call | solution.py:214
  390.8 4.1 copy.70
  394.8 3.8 all-to-all-start.1
  400.6 18.5 %all-to-all-done.1 = bf16[20,64,720]{2,0,1:T(8,128)(2,1)S(1)} async-done(((bf16[20,64,720]{2,0,1:T(8,128)(2,1)}), bf16[20,64,720]{2,0,1:T(8,128)(2,1)S(1)}, u32[]{:S(2)}, u32[]{:S(2)}) %all-to-all-start.1) | async-done | bytes 1843232 | tf_op jit(solution)/shard_map/all_to_all | solution.py:327
  419.1 3.3 copy.79
  422.4 4.8 reshape.39
  427.3 5.4 fusion.28
  432.7 3.3 add_multiply_fusion
  436.1 3.9 fusion.12
  440.0 3.9 fusion.20
  444.0 6.2 %add_add_fusion = f32[640,1440]{0,1:T(8,128)} fusion(f32[640,1440]{0,1:T(8,128)S(1)} %fusion.20, f32[640,1440]{0,1:T(8,128)S(1)} %fusion.12, bf16[1536,1440]{1,0:T(8,128)(2,1)S(1)} %bitcast.88, f32[640,1536]{1,0:T(8,128)S(1)} %add_multiply_fusion), kind=kOutput, calls=%fused_computation.38 | convolution fusion | flops 2834964480 | bytes 19415040 | tf_op jit(solution)/shard_map/dot_general | solution.py:59
  450.2 5.2 copy.72
  455.4 8.6 %multiply_reduce_fusion.3 = (f32[]{:T(128)}, f32[32,20,1440]{2,0,1:T(8,128)}, f32[]{:T(128)}, f32[]{:T(128)}) fusion(f32[32,20,1440]{2,0,1:T(8,128)} %param.24, f32[32,20,1440]{2,0,1:T(8,128)} %bitcast.68, f32[32,20,1440]{2,0,1:T(8,128)} %param.40), kind=kLoop, calls=%fused_computation.37 | loop fusion | flops 6451197 | bytes 14745612 | tf_op jit(solution)/shard_map/reduce_sum | solution.py:330
  464.6 63.1 %all-reduce.1 = (f32[]{:T(128)}, f32[]{:T(128)}, f32[]{:T(128)}) all-reduce(f32[]{:T(128)} %get-tuple-element.10, f32[]{:T(128)} %get-tuple-element.23, f32[]{:T(128)S(6)} %add.74), channel_id=1, replica_groups=mesh['grp'=2,'lat'=8,'lon'=2] {'grp','lat','lon'}, use_global_device_ids=true, to_apply=%region_3.4 | all-reduce | flops 3 | bytes 24 | tf_op jit(solution)/shard_map/psum | solution.py:330
  529.6 6.4 %multiply_add_fusion = f32[32,20,1440]{2,0,1:T(8,128)} fusion(f32[32,20,1440]{2,0,1:T(8,128)} %param.41, f32[32,20,1440]{2,0,1:T(8,128)} %get-tuple-element.11, f32[]{:T(128)S(6)} %div.6), kind=kLoop, calls=%fused_computation.35 | loop fusion | flops 2764800 | bytes 11059204 | tf_op jit(solution)/shard_map/add | solution.py:333
  (96 shorter events, 7.4 us)
Async XLA Ops:
  0.6 1.9 copy-start
  10.9 8.5 %slice-start.12 = ((s8[4423680]{0:T(1024)(128)(4,1)}), s8[229376]{0:T(1024)(128)(4,1)S(1)}, s32[]{:S(2)}) async-start(s8[4423680]{0:T(1024)(128)(4,1)} %bitcast.97), calls=%async_computation.14 | async-start | bytes 458752
  16.5 3.4 slice-start.13
  19.9 11.6 %slice-start.8 = ((s8[4423680]{0:T(1024)(128)(4,1)}), s8[4194304]{0:T(1024)(128)(4,1)S(1)}, s32[]{:S(2)}) async-start(s8[4423680]{0:T(1024)(128)(4,1)} %bitcast.93), calls=%async_computation.10 | async-start | bytes 8388608
  25.7 5.8 %copy-start.9 = (f32[640,1536]{0,1:T(8,128)S(1)}, f32[640,1536]{0,1:T(8,128)}, u32[]{:S(2)}) copy-start(f32[640,1536]{0,1:T(8,128)} %copy.64) | copy-start | bytes 11796484
  25.7 5.8 %slice-start.9 = ((s8[4423680]{0:T(1024)(128)(4,1)}), s8[229376]{0:T(1024)(128)(4,1)S(1)}, s32[]{:S(2)}) async-start(s8[4423680]{0:T(1024)(128)(4,1)} %bitcast.93), calls=%async_computation.11 | async-start | bytes 458752
  25.7 13.1 %slice-start.4 = ((s8[4718592]{0:T(1024)(128)(4,1)}), s8[4194304]{0:T(1024)(128)(4,1)S(1)}, s32[]{:S(2)}) async-start(s8[4718592]{0:T(1024)(128)(4,1)} %bitcast.89), calls=%async_computation.6 | async-start | bytes 8388608
  31.5 7.4 %slice-start.5 = ((s8[4718592]{0:T(1024)(128)(4,1)}), s8[524288]{0:T(1024)(128)(4,1)S(1)}, s32[]{:S(2)}) async-start(s8[4718592]{0:T(1024)(128)(4,1)} %bitcast.89), calls=%async_computation.7 | async-start | bytes 1048576
  31.5 17.1 %slice-start = ((s8[4718592]{0:T(1024)(128)(4,1)}), s8[4194304]{0:T(1024)(128)(4,1)S(1)}, s32[]{:S(2)}) async-start(s8[4718592]{0:T(1024)(128)(4,1)} %bitcast.85), calls=%async_computation.2 | async-start | bytes 8388608
  38.9 9.8 %slice-start.1 = ((s8[4718592]{0:T(1024)(128)(4,1)}), s8[524288]{0:T(1024)(128)(4,1)S(1)}, s32[]{:S(2)}) async-start(s8[4718592]{0:T(1024)(128)(4,1)} %bitcast.85), calls=%async_computation.3 | async-start | bytes 1048576
  58.4 27.4 %all-to-all-start = ((bf16[2,20,32,720]{3,2,1,0:T(8,128)(2,1)}), bf16[2,20,32,720]{3,2,1,0:T(8,128)(2,1)S(1)}, u32[]{:S(2)}, u32[]{:S(2)}) async-start(bf16[2,20,32,720]{3,2,1,0:T(8,128)(2,1)} %pad_maximum_fusion.1), calls=%async_computation | async-start | bytes 3932160 | tf_op jit(solution)/shard_map/all_to_all | solution.py:302
  62.1 7.3 %copy-start.7 = (bf16[64,20,720]{2,0,1:T(8,128)(2,1)S(1)}, bf16[64,20,720]{2,0,1:T(8,128)(2,1)}, u32[]{:S(2)}) copy-start(bf16[64,20,720]{2,0,1:T(8,128)(2,1)} %param.30) | copy-start | bytes 5529604
  62.1 8.4 %copy-start.13 = (s32[2]{0:T(128)S(1)}, s32[2]{0:T(128)}, u32[]{:S(2)}) copy-start(s32[2]{0:T(128)} %param.28) | copy-start | bytes 28
  62.1 9.0 %copy-start.14 = (f32[4]{0:T(128)S(1)}, f32[4]{0:T(128)}, u32[]{:S(2)}) copy-start(f32[4]{0:T(128)} %param.35) | copy-start | bytes 52
  62.2 9.7 %copy-start.11 = (bf16[256,64]{0,1:T(8,128)(2,1)S(1)}, bf16[256,64]{0,1:T(8,128)(2,1)}, u32[]{:S(2)}) copy-start(bf16[256,64]{0,1:T(8,128)(2,1)} %param.34) | copy-start | bytes 98308
  62.2 12.9 %copy-start.10 = (bf16[64,256]{1,0:T(8,128)(2,1)S(1)}, bf16[64,256]{1,0:T(8,128)(2,1)}, u32[]{:S(2)}) copy-start(bf16[64,256]{1,0:T(8,128)(2,1)} %vw.1) | copy-start | bytes 98308
  64.9 91.5 %collective-permute-start.6 = (bf16[10,64,720]{2,1,0:T(8,128)(2,1)}, bf16[10,64,720]{2,1,0:T(8,128)(2,1)}, u32[]{:S(2)}, u32[]{:S(2)}) collective-permute-start(bf16[10,64,720]{2,1,0:T(8,128)(2,1)} %slice.118), channel_id=1, source_target_pairs={{0,30},{2,0},{4,2},{6,4},{8,6},{10,8},{12,10},{14,12},{16,14},{18,... | collective-permute-start | bytes 2764808 | tf_op jit(solution)/shard_map/ppermute | solution.py:25
  68.0 91.0 %collective-permute-start.4 = (bf16[10,64,720]{2,1,0:T(8,128)(2,1)}, bf16[10,64,720]{2,1,0:T(8,128)(2,1)}, u32[]{:S(2)}, u32[]{:S(2)}) collective-permute-start(bf16[10,64,720]{2,1,0:T(8,128)(2,1)} %slice.119), channel_id=1, source_target_pairs={{0,30},{2,0},{4,2},{6,4},{8,6},{10,8},{12,10},{14,12},{16,14},{18,... | collective-permute-start | bytes 2764808 | tf_op jit(solution)/shard_map/ppermute | solution.py:25
  70.5 92.5 %collective-permute-start = (bf16[10,64,720]{2,1,0:T(8,128)(2,1)}, bf16[10,64,720]{2,1,0:T(8,128)(2,1)S(1)}, u32[]{:S(2)}, u32[]{:S(2)}) collective-permute-start(bf16[10,64,720]{2,1,0:T(8,128)(2,1)} %slice.93), channel_id=1, source_target_pairs={{0,30},{2,0},{4,2},{6,4},{8,6},{10,8},{12,10},{14,12},{16,14},{18,... | collective-permute-start | bytes 2764808 | tf_op jit(solution)/shard_map/ppermute | solution.py:25
  153.9 3.9 copy-start.5
  155.7 28.8 %collective-permute-start.2 = (bf16[10,64,720]{2,1,0:T(8,128)(2,1)S(1)}, bf16[10,64,720]{2,1,0:T(8,128)(2,1)S(1)}, u32[]{:S(2)}, u32[]{:S(2)}) collective-permute-start(bf16[10,64,720]{2,1,0:T(8,128)(2,1)S(1)} %slice.120), channel_id=1, source_target_pairs={{0,30},{2,0},{4,2},{6,4},{8,6},{10,8},{12,10},{14,12},{16,14},{18,... | collective-permute-start | bytes 2764808 | tf_op jit(solution)/shard_map/ppermute | solution.py:25
  157.8 2.6 copy-start.6
  158.6 10.7 %collective-permute-start.7 = (bf16[20,64,10]{2,1,0:T(8,128)(2,1)S(1)}, bf16[20,64,10]{2,1,0:T(8,128)(2,1)S(1)}, u32[]{:S(2)}, u32[]{:S(2)}) collective-permute-start(bf16[20,64,10]{2,1,0:T(8,128)(2,1)S(1)} %slice.122), channel_id=1, source_target_pairs={{0,1},{1,0},{2,3},{3,2},{4,5},{5,4},{6,7},{7,6},{8,9},{9,8},{10,11... | collective-permute-start | bytes 76808 | tf_op jit(solution)/shard_map/ppermute | solution.py:25
  160.4 2.6 copy-start.8
  161.2 15.1 %collective-permute-start.5 = (bf16[20,64,10]{2,1,0:T(8,128)(2,1)S(1)}, bf16[20,64,10]{2,1,0:T(8,128)(2,1)S(1)}, u32[]{:S(2)}, u32[]{:S(2)}) collective-permute-start(bf16[20,64,10]{2,1,0:T(8,128)(2,1)S(1)} %slice.123), channel_id=1, source_target_pairs={{0,1},{1,0},{2,3},{3,2},{4,5},{5,4},{6,7},{7,6},{8,9},{9,8},{10,11... | collective-permute-start | bytes 76808 | tf_op jit(solution)/shard_map/ppermute | solution.py:25
  163.7 22.1 %collective-permute-start.1 = (bf16[20,64,10]{2,1,0:T(8,128)(2,1)S(1)}, bf16[20,64,10]{2,1,0:T(8,128)(2,1)S(1)}, u32[]{:S(2)}, u32[]{:S(2)}) collective-permute-start(bf16[20,64,10]{2,1,0:T(8,128)(2,1)S(1)} %slice.94), channel_id=1, source_target_pairs={{0,1},{1,0},{2,3},{3,2},{4,5},{5,4},{6,7},{7,6},{8,9},{9,8},{10,11... | collective-permute-start | bytes 76808 | tf_op jit(solution)/shard_map/ppermute | solution.py:25
  180.4 4.2 copy-start.2
  185.4 7.1 %collective-permute-start.3 = (bf16[20,64,10]{2,1,0:T(8,128)(2,1)S(1)}, bf16[20,64,10]{2,1,0:T(8,128)(2,1)S(1)}, u32[]{:S(2)}, u32[]{:S(2)}) collective-permute-start(bf16[20,64,10]{2,1,0:T(8,128)(2,1)S(1)} %slice.124), channel_id=1, source_target_pairs={{0,1},{1,0},{2,3},{3,2},{4,5},{5,4},{6,7},{7,6},{8,9},{9,8},{10,11... | collective-permute-start | bytes 76808 | tf_op jit(solution)/shard_map/ppermute | solution.py:25
  290.8 18.2 %collective-permute-start.8 = (bf16[10,64,720]{2,1,0:T(8,128)(2,1)S(1)}, bf16[10,64,720]{2,1,0:T(8,128)(2,1)S(1)}, u32[]{:S(2)}, u32[]{:S(2)}) collective-permute-start(bf16[10,64,720]{2,1,0:T(8,128)(2,1)S(1)} %slice.117), channel_id=1, source_target_pairs={{0,2},{2,4},{4,6},{6,8},{8,10},{10,12},{12,14},{14,16},{16,18},{18... | collective-permute-start | bytes 2764808 | tf_op jit(solution)/shard_map/ppermute | solution.py:25
  311.2 1.9 copy-start.3
  313.2 7.1 %collective-permute-start.9 = (bf16[20,64,10]{2,1,0:T(8,128)(2,1)S(1)}, bf16[20,64,10]{2,1,0:T(8,128)(2,1)S(1)}, u32[]{:S(2)}, u32[]{:S(2)}) collective-permute-start(bf16[20,64,10]{2,1,0:T(8,128)(2,1)S(1)} %slice.121), channel_id=1, source_target_pairs={{0,1},{1,0},{2,3},{3,2},{4,5},{5,4},{6,7},{7,6},{8,9},{9,8},{10,11... | collective-permute-start | bytes 76808 | tf_op jit(solution)/shard_map/ppermute | solution.py:25
  390.7 7.9 %copy-start.12 = (f32[448,64]{1,0:T(8,128)S(1)}, f32[448,64]{1,0:T(8,128)}, u32[]{:S(2)}) copy-start(f32[448,64]{1,0:T(8,128)} %get-tuple-element.6) | copy-start | bytes 344068
  394.8 24.3 %all-to-all-start.1 = ((bf16[20,64,720]{2,0,1:T(8,128)(2,1)}), bf16[20,64,720]{2,0,1:T(8,128)(2,1)S(1)}, u32[]{:S(2)}, u32[]{:S(2)}) async-start(bf16[20,64,720]{2,0,1:T(8,128)(2,1)} %copy.70), calls=%async_computation.1 | async-start | bytes 4718592 | tf_op jit(solution)/shard_map/all_to_all | solution.py:327
  419.1 13.6 %slice-start.10 = ((s8[4423680]{0:T(1024)(128)(4,1)}), s8[229376]{0:T(1024)(128)(4,1)S(1)}, s32[]{:S(2)}) async-start(s8[4423680]{0:T(1024)(128)(4,1)} %bitcast.95), calls=%async_computation.12 | async-start | bytes 458752
  427.2 5.4 %copy-start.4 = (f32[20,32,1536]{2,1,0:T(8,128)S(1)}, f32[20,32,1536]{2,1,0:T(8,128)}, u32[]{:S(2)}) copy-start(f32[20,32,1536]{2,1,0:T(8,128)} %copy.63) | copy-start | bytes 11796484
  427.2 5.4 %slice-start.11 = ((s8[4423680]{0:T(1024)(128)(4,1)}), s8[4194304]{0:T(1024)(128)(4,1)S(1)}, s32[]{:S(2)}) async-start(s8[4423680]{0:T(1024)(128)(4,1)} %bitcast.95), calls=%async_computation.13 | async-start | bytes 8388608
  427.3 8.8 %slice-start.6 = ((s8[4718592]{0:T(1024)(128)(4,1)}), s8[4194304]{0:T(1024)(128)(4,1)S(1)}, s32[]{:S(2)}) async-start(s8[4718592]{0:T(1024)(128)(4,1)} %bitcast.91), calls=%async_computation.8 | async-start | bytes 8388608
  432.7 3.3 slice-start.7
  432.7 11.2 %slice-start.2 = ((s8[4718592]{0:T(1024)(128)(4,1)}), s8[4194304]{0:T(1024)(128)(4,1)S(1)}, s32[]{:S(2)}) async-start(s8[4718592]{0:T(1024)(128)(4,1)} %bitcast.87), calls=%async_computation.4 | async-start | bytes 8388608
  436.0 7.9 %slice-start.3 = ((s8[4718592]{0:T(1024)(128)(4,1)}), s8[524288]{0:T(1024)(128)(4,1)S(1)}, s32[]{:S(2)}) async-start(s8[4718592]{0:T(1024)(128)(4,1)} %bitcast.87), calls=%async_computation.5 | async-start | bytes 1048576
  529.6 6.4 %copy-start.1 = (f32[24,32,721]{2,1,0:T(8,128)S(1)}, f32[24,32,721]{2,1,0:T(8,128)}, u32[]{:S(2)}) copy-start(f32[24,32,721]{2,1,0:T(8,128)} %param.25) | copy-start | bytes 6644740
